TPU v7x, 128 devices: a whole 4x4x4 slice. The times are simulated.
128 devices in a mesh: region: 16 (over x, y_lo, core), patch: 8 (over z, y_hi).
Axes of the slice: x: 4, y: 4 (y_hi: 2, y_lo: 2; y = y_hi * 2 + y_lo), z: 4, core: 2. Of those that a mesh axis runs over, the one named last changes fastest.
Arguments:
- coarse_state: float32 [12, 256, 256], P(None, ('region', 'patch')), may hold values from -6 to 6
- anchors: int32 [256, 2], P('region'), may hold values from 0 to 1920, as said below
- region_count: int32 [16], P('region'), may hold values from 8 to 16, as said below
- blend: int32 [256], P('region'), may hold values from 1 to 4
- w_in: bfloat16 [3, 3, 16, 128], replicated, may hold values from -0.5 to 0.5
- b_in: float32 [128], replicated, may hold values from -4 to 4
- gamma: float32 [128], replicated, may hold values from 0.1 to 1.9
- beta: float32 [128], replicated, may hold values from -3 to 3
- w_mid: bfloat16 [3, 3, 128, 128], replicated, may hold values from -0.1875 to 0.1875
- w_out: bfloat16 [3, 3, 128, 12], replicated, may hold values from -0.1875 to 0.1875
Outputs:
- downscaled: float32 [12, 2048, 2048], P(None, 'region', 'patch')
Inputs may be any that keep to these rules, and one draw needn't show every extreme that they name: `anchors`: rows r * 16 to r * 16 + 15 belong to region r. The first entry is the patch's top row: at least r * 128 and at most r * 128 + 128 / 2; the second is its left column; every patch of 128 x 128 cells lies inside the grid. The first region_count[r] slots of region r are live; some region has all 16 slots live.
All inputs are finite; a program needn't handle non-finite values.
Results may differ from a plain program's by a relative error of at most 0.006.
Values may be sent and summed in bfloat16 or wider, within the bound.
A program may use at most 192 MiB of HBM per device.

v0:
```python
from functools import partial
import math

import jax
import jax.numpy as jnp
from jax import lax
from jax.sharding import PartitionSpec as P

VARS = 12
GROUPS = 32
PS = 128
F = 8
TH = 128
TW = 256


def with_halo(shard, sides, width):
    for axis, dim in sides:
        count, length = (lax.axis_size(axis), shard.shape[dim])
        up = [(i, (i + 1) % count) for i in range(count - 1)]
        down = [(j, i) for i, j in up]
        last = lax.slice_in_dim(shard, length - width, length, axis=dim)
        leading = lax.slice_in_dim(shard, 0, width, axis=dim)
        before = lax.ppermute(last, axis, up)
        after = lax.ppermute(leading, axis, down)
        shard = jnp.concatenate([before, shard, after], axis=dim)
    return shard


def as_sent(shard):
    return jax.tree.map(lambda a: a.astype(jnp.bfloat16) if a.dtype == jnp.float32 else a, shard)


def passed_along(value, axis, steps):
    count = lax.axis_size(axis)
    leading, last = (max(0, -steps), min(count, count - steps))
    return lax.ppermute(value, axis, [(source, source + steps) for source in range(leading, last)])


def hat_table(start_cell, length, coarse_limit, start_coarse, table_width):
    fine_index = start_cell.astype(jnp.float32) + jnp.arange(length).astype(jnp.float32)
    location = jnp.clip((fine_index + 0.5) / F - 0.5, 0.0, coarse_limit - 1.0)
    coarse_index = start_coarse.astype(jnp.float32) + jnp.arange(table_width).astype(jnp.float32)
    return jnp.maximum(0.0, 1.0 - jnp.abs(location[:, None] - coarse_index[None, :]))


def conv_same(inputs, kernel):
    return lax.conv_general_dilated(
        inputs,
        kernel,
        (1, 1),
        "SAME",
        dimension_numbers=("NHWC", "HWIO", "NHWC"),
        preferred_element_type=jnp.float32,
    )


def group_act(first_act, gamma, beta):
    channels = first_act.shape[3]
    values = first_act.astype(jnp.float32).reshape(
        first_act.shape[1] * first_act.shape[2], GROUPS, channels // GROUPS
    )
    group_mean = jnp.mean(values, axis=(0, 2), keepdims=True)
    centred = values - group_mean
    group_var = jnp.mean(centred * centred, axis=(0, 2), keepdims=True)
    normed = (centred / jnp.sqrt(group_var + 1e-05)).reshape(first_act.shape)
    return jax.nn.silu(normed * gamma + beta).astype(jnp.bfloat16)


def unet_patch(coarse_rows, row_base, coarse_limit, height, breadth, anchor_y, anchor_x, weights):
    w_in, b_in, gamma, beta, w_mid, w_out = weights
    window = PS // F + 3
    column_limit = coarse_rows.shape[2]
    row_start = jnp.clip(anchor_y // F - 1, 0, coarse_limit - window)
    col_start = jnp.clip(anchor_x // F - 1, 0, column_limit - window)
    local_row = row_start - row_base
    patch_coarse = lax.dynamic_slice(
        coarse_rows, (jnp.int32(0), local_row, col_start), (coarse_rows.shape[0], window, window)
    )
    table_y = hat_table(anchor_y, PS, coarse_limit, row_start, window)
    table_x = hat_table(anchor_x, PS, column_limit, col_start, window)
    half_done = jnp.einsum("ic,vcd->ivd", table_y, patch_coarse, precision=lax.Precision.HIGHEST)
    interp = jnp.einsum("ivd,jd->ijv", half_done, table_x, precision=lax.Precision.HIGHEST)
    angle_y = (anchor_y.astype(jnp.float32) + jnp.arange(PS).astype(jnp.float32)) * (
        2.0 * math.pi / height
    )
    angle_x = (anchor_x.astype(jnp.float32) + jnp.arange(PS).astype(jnp.float32)) * (
        2.0 * math.pi / breadth
    )
    patch_shape = (PS, PS)
    position = jnp.stack(
        [
            jnp.broadcast_to(jnp.sin(angle_y)[:, None], patch_shape),
            jnp.broadcast_to(jnp.cos(angle_y)[:, None], patch_shape),
            jnp.broadcast_to(jnp.sin(angle_x)[None, :], patch_shape),
            jnp.broadcast_to(jnp.cos(angle_x)[None, :], patch_shape),
        ],
        axis=2,
    )
    inputs = jnp.concatenate([interp, position], axis=2).astype(jnp.bfloat16)[None]
    first_act = (conv_same(inputs, w_in) + b_in).astype(jnp.bfloat16)
    norm_act = group_act(first_act, gamma, beta)
    second = (first_act.astype(jnp.float32) + conv_same(norm_act, w_mid)).astype(jnp.bfloat16)
    result = (conv_same(second, w_out)[0] + interp).astype(jnp.bfloat16)
    return jnp.transpose(result, (2, 0, 1))


def place_patch(
    totals, produced, slot_ident, is_live, anchors, blend, row_shift, col_shift, inner_width
):
    numerator, cover = totals
    anchor_y = anchors[slot_ident, 0] - row_shift
    anchor_x = anchors[slot_ident, 1] - col_shift + PS
    inside = is_live & (anchor_x > 0) & (anchor_x < inner_width + PS)
    column_at = jnp.clip(anchor_x, 0, inner_width + PS)
    blend_scale = jnp.where(inside, blend[slot_ident], 0).astype(jnp.float32)
    corner = (jnp.int32(0), anchor_y, column_at)
    current = lax.dynamic_slice(numerator, corner, (VARS, PS, PS))
    numerator = lax.dynamic_update_slice(
        numerator, current + blend_scale * produced.astype(jnp.float32), corner
    )
    covered = lax.dynamic_slice(cover, corner, (1, PS, PS))
    cover = lax.dynamic_update_slice(cover, covered + blend_scale, corner)
    return (numerator, cover)


def per_device(coarse_state, anchors, region_count, blend, w_in, b_in, gamma, beta, w_mid, w_out):
    weights = (w_in, b_in, gamma, beta, w_mid, w_out)
    n_region = lax.axis_size("region")
    n_patch = lax.axis_size("patch")
    region = lax.axis_index("region")
    column = lax.axis_index("patch")
    coarse_limit = coarse_state.shape[1] * n_region * n_patch
    band_rows = coarse_limit // n_region
    height = TH * n_region
    breadth = TW * n_patch
    slot_count = anchors.shape[0] // n_patch
    live_count = region_count[0]
    within = lax.all_gather(coarse_state, "patch", axis=1, tiled=True)
    coarse_rows = with_halo(within, (("region", 1),), band_rows)
    row_base = (region - 1) * band_rows

    def slot_of(device, slot_index):
        return device * slot_count + slot_index

    def run_slot(slot_index):
        slot_ident = slot_of(column, slot_index)
        anchor_y = anchors[slot_ident, 0]
        anchor_x = anchors[slot_ident, 1]
        return lax.cond(
            slot_ident < live_count,
            partial(
                unet_patch,
                coarse_rows,
                row_base,
                coarse_limit,
                height,
                breadth,
                anchor_y,
                anchor_x,
                weights,
            ),
            partial(jnp.zeros, (VARS, PS, PS), jnp.bfloat16),
        )

    produced = lax.map(run_slot, jnp.arange(slot_count))
    empty_sums = (
        jnp.zeros((VARS, 2 * TH, TW + 2 * PS), jnp.float32),
        jnp.zeros((1, 2 * TH, TW + 2 * PS), jnp.float32),
    )
    piece = jax.tree.map(
        lambda part: lax.all_gather(part, "patch", axis=0, tiled=True), as_sent(produced)
    )

    def absorb_one(offset, running):
        slot_ident = slot_of(offset // slot_count, offset % slot_count)
        return place_patch(
            running,
            piece[offset],
            slot_ident,
            slot_ident < live_count,
            anchors,
            blend,
            region * TH,
            column * TW,
            TW,
        )

    numerator, cover = lax.fori_loop(0, piece.shape[0], absorb_one, empty_sums)
    numerator = numerator[:, :, PS : PS + TW]
    cover = cover[:, :, PS : PS + TW]
    below_numerator, below_cover = (
        passed_along(numerator[:, TH:].astype(jnp.bfloat16), "region", 1).astype(jnp.float32),
        passed_along(cover[:, TH:].astype(jnp.bfloat16), "region", 1).astype(jnp.float32),
    )
    numerator = numerator[:, :TH] + below_numerator
    cover = cover[:, :TH] + below_cover
    return numerator / jnp.maximum(cover, 1.0)


def solution(mesh):
    return jax.shard_map(
        per_device,
        mesh=mesh,
        in_specs=(
            P(None, ("region", "patch"), None),
            P("region", None),
            P("region"),
            P("region"),
            P(),
            P(),
            P(),
            P(),
            P(),
            P(),
        ),
        out_specs=P(None, "region", "patch"),
        check_vma=False,
    )
```

profile of v0, /device:TPU:104, one launch (start us, length us, event | category | flops | bytes accessed | tf_op | source)
XLA Modules:
  0.0 583.5 jit_solution(5252626039697528841)
XLA Ops:
  7.3 32.6 %all_gather.6 = f32[12,16,256]{2,0,1:T(8,128)S(1)} all-gather(f32[12,2,256]{2,0,1:T(8,128)S(1)} %copy.23), channel_id=1, replica_groups=mesh['region'=16,'patch'=8] {'patch'}, dimensions={1}, use_global_device_ids=true | all-gather | bytes 221184 | tf_op jit(solution)/shard_map/all_gather | solution.py:139
  45.7 4.6 collective-permute-done
  52.0 6.2 %while.29 = (s32[]{:T(128)}, bf16[2,12,128,128]{3,2,1,0:T(8,128)(2,1)}, s32[2]{0:T(128)S(1)}, s32[]{:T(128)}, s32[]{:T(128)}, /*index=5*/s32[16,2]{0,1:T(2,128)}...) while((s32[]{:T(128)}, ...), condition=%wide.region_7.8_spmd, body=%wide.region_0.7_spmd.sunk | while | flops 6385967104 | bytes 68353440 | solution.py:166
  58.3 227.2 %all-gather.2.cloned.1.call-done = bf16[16,12,128,128]{3,2,1,0:T(8,128)(2,1)} async-done(((bf16[2,12,128,128]{3,2,1,0:T(8,128)(2,1)}), bf16[16,12,128,128]{3,2,1,0:T(8,128)(2,1)}) %all-gather.2.cloned.1.call-update) | async-done | bytes 6291472 | tf_op jit(solution)/shard_map/all_gather | solution.py:172
  285.6 3.4 broadcast_in_dim.24
  289.0 269.3 %while.30 = (s32[]{:T(128)}, f32[12,256,512]{2,1,0:T(8,128)}, f32[1,256,512]{2,1,0:T(8,128)S(1)}, s32[16,2]{0,1:T(2,128)S(1)}, s32[]{:T(128)}, /*index=5*/s32[]{...) while((s32[]{:T(128)}, f32[12,256,512]{2,1,0:T(8,128)}, ...), condition=%wide.region_9.10_spmd, body=%wide.region_8.9_spmd.sunk | while | flops 606242 | bytes 3801642 | solution.py:189
  296.7 10.8 %dynamic_update_slice.31 = f32[12,256,512]{2,1,0:T(8,128)} dynamic-update-slice(f32[12,256,512]{2,1,0:T(8,128)} %get-tuple-element.788, f32[12,128,128]{2,1,0:T(8,128)S(1)} %bitcast_add_fusion.2, s32[]{:T(128)} %constant.246.clone.1..sunk, s32[]{:T(128)S(6)} %select_n.116, s32[]{:T(128)S(6)} %min.38) | dynamic-update-slice | bytes 1572868 | tf_op jit(solution)/shard_map/while/body/eval_jaxpr/dynamic_update_slice | solution.py:119
  314.7 8.4 %dynamic_update_slice.31 = f32[12,256,512]{2,1,0:T(8,128)} dynamic-update-slice(f32[12,256,512]{2,1,0:T(8,128)} %get-tuple-element.788, f32[12,128,128]{2,1,0:T(8,128)S(1)} %bitcast_add_fusion.2, s32[]{:T(128)} %constant.246.clone.1..sunk, s32[]{:T(128)S(6)} %select_n.116, s32[]{:T(128)S(6)} %min.38) | dynamic-update-slice | bytes 1572868 | tf_op jit(solution)/shard_map/while/body/eval_jaxpr/dynamic_update_slice | solution.py:119
  330.4 8.5 %dynamic_update_slice.31 = f32[12,256,512]{2,1,0:T(8,128)} dynamic-update-slice(f32[12,256,512]{2,1,0:T(8,128)} %get-tuple-element.788, f32[12,128,128]{2,1,0:T(8,128)S(1)} %bitcast_add_fusion.2, s32[]{:T(128)} %constant.246.clone.1..sunk, s32[]{:T(128)S(6)} %select_n.116, s32[]{:T(128)S(6)} %min.38) | dynamic-update-slice | bytes 1572868 | tf_op jit(solution)/shard_map/while/body/eval_jaxpr/dynamic_update_slice | solution.py:119
  346.2 8.4 %dynamic_update_slice.31 = f32[12,256,512]{2,1,0:T(8,128)} dynamic-update-slice(f32[12,256,512]{2,1,0:T(8,128)} %get-tuple-element.788, f32[12,128,128]{2,1,0:T(8,128)S(1)} %bitcast_add_fusion.2, s32[]{:T(128)} %constant.246.clone.1..sunk, s32[]{:T(128)S(6)} %select_n.116, s32[]{:T(128)S(6)} %min.38) | dynamic-update-slice | bytes 1572868 | tf_op jit(solution)/shard_map/while/body/eval_jaxpr/dynamic_update_slice | solution.py:119
  362.4 11.0 %dynamic_update_slice.31 = f32[12,256,512]{2,1,0:T(8,128)} dynamic-update-slice(f32[12,256,512]{2,1,0:T(8,128)} %get-tuple-element.788, f32[12,128,128]{2,1,0:T(8,128)S(1)} %bitcast_add_fusion.2, s32[]{:T(128)} %constant.246.clone.1..sunk, s32[]{:T(128)S(6)} %select_n.116, s32[]{:T(128)S(6)} %min.38) | dynamic-update-slice | bytes 1572868 | tf_op jit(solution)/shard_map/while/body/eval_jaxpr/dynamic_update_slice | solution.py:119
  380.7 8.5 %dynamic_update_slice.31 = f32[12,256,512]{2,1,0:T(8,128)} dynamic-update-slice(f32[12,256,512]{2,1,0:T(8,128)} %get-tuple-element.788, f32[12,128,128]{2,1,0:T(8,128)S(1)} %bitcast_add_fusion.2, s32[]{:T(128)} %constant.246.clone.1..sunk, s32[]{:T(128)S(6)} %select_n.116, s32[]{:T(128)S(6)} %min.38) | dynamic-update-slice | bytes 1572868 | tf_op jit(solution)/shard_map/while/body/eval_jaxpr/dynamic_update_slice | solution.py:119
  396.9 10.9 %dynamic_update_slice.31 = f32[12,256,512]{2,1,0:T(8,128)} dynamic-update-slice(f32[12,256,512]{2,1,0:T(8,128)} %get-tuple-element.788, f32[12,128,128]{2,1,0:T(8,128)S(1)} %bitcast_add_fusion.2, s32[]{:T(128)} %constant.246.clone.1..sunk, s32[]{:T(128)S(6)} %select_n.116, s32[]{:T(128)S(6)} %min.38) | dynamic-update-slice | bytes 1572868 | tf_op jit(solution)/shard_map/while/body/eval_jaxpr/dynamic_update_slice | solution.py:119
  415.1 8.3 %dynamic_update_slice.31 = f32[12,256,512]{2,1,0:T(8,128)} dynamic-update-slice(f32[12,256,512]{2,1,0:T(8,128)} %get-tuple-element.788, f32[12,128,128]{2,1,0:T(8,128)S(1)} %bitcast_add_fusion.2, s32[]{:T(128)} %constant.246.clone.1..sunk, s32[]{:T(128)S(6)} %select_n.116, s32[]{:T(128)S(6)} %min.38) | dynamic-update-slice | bytes 1572868 | tf_op jit(solution)/shard_map/while/body/eval_jaxpr/dynamic_update_slice | solution.py:119
  431.1 10.8 %dynamic_update_slice.31 = f32[12,256,512]{2,1,0:T(8,128)} dynamic-update-slice(f32[12,256,512]{2,1,0:T(8,128)} %get-tuple-element.788, f32[12,128,128]{2,1,0:T(8,128)S(1)} %bitcast_add_fusion.2, s32[]{:T(128)} %constant.246.clone.1..sunk, s32[]{:T(128)S(6)} %select_n.116, s32[]{:T(128)S(6)} %min.38) | dynamic-update-slice | bytes 1572868 | tf_op jit(solution)/shard_map/while/body/eval_jaxpr/dynamic_update_slice | solution.py:119
  449.2 8.4 %dynamic_update_slice.31 = f32[12,256,512]{2,1,0:T(8,128)} dynamic-update-slice(f32[12,256,512]{2,1,0:T(8,128)} %get-tuple-element.788, f32[12,128,128]{2,1,0:T(8,128)S(1)} %bitcast_add_fusion.2, s32[]{:T(128)} %constant.246.clone.1..sunk, s32[]{:T(128)S(6)} %select_n.116, s32[]{:T(128)S(6)} %min.38) | dynamic-update-slice | bytes 1572868 | tf_op jit(solution)/shard_map/while/body/eval_jaxpr/dynamic_update_slice | solution.py:119
  465.0 8.5 %dynamic_update_slice.31 = f32[12,256,512]{2,1,0:T(8,128)} dynamic-update-slice(f32[12,256,512]{2,1,0:T(8,128)} %get-tuple-element.788, f32[12,128,128]{2,1,0:T(8,128)S(1)} %bitcast_add_fusion.2, s32[]{:T(128)} %constant.246.clone.1..sunk, s32[]{:T(128)S(6)} %select_n.116, s32[]{:T(128)S(6)} %min.38) | dynamic-update-slice | bytes 1572868 | tf_op jit(solution)/shard_map/while/body/eval_jaxpr/dynamic_update_slice | solution.py:119
  480.9 8.5 %dynamic_update_slice.31 = f32[12,256,512]{2,1,0:T(8,128)} dynamic-update-slice(f32[12,256,512]{2,1,0:T(8,128)} %get-tuple-element.788, f32[12,128,128]{2,1,0:T(8,128)S(1)} %bitcast_add_fusion.2, s32[]{:T(128)} %constant.246.clone.1..sunk, s32[]{:T(128)S(6)} %select_n.116, s32[]{:T(128)S(6)} %min.38) | dynamic-update-slice | bytes 1572868 | tf_op jit(solution)/shard_map/while/body/eval_jaxpr/dynamic_update_slice | solution.py:119
  496.6 8.3 %dynamic_update_slice.31 = f32[12,256,512]{2,1,0:T(8,128)} dynamic-update-slice(f32[12,256,512]{2,1,0:T(8,128)} %get-tuple-element.788, f32[12,128,128]{2,1,0:T(8,128)S(1)} %bitcast_add_fusion.2, s32[]{:T(128)} %constant.246.clone.1..sunk, s32[]{:T(128)S(6)} %select_n.116, s32[]{:T(128)S(6)} %min.38) | dynamic-update-slice | bytes 1572868 | tf_op jit(solution)/shard_map/while/body/eval_jaxpr/dynamic_update_slice | solution.py:119
  512.3 8.5 %dynamic_update_slice.31 = f32[12,256,512]{2,1,0:T(8,128)} dynamic-update-slice(f32[12,256,512]{2,1,0:T(8,128)} %get-tuple-element.788, f32[12,128,128]{2,1,0:T(8,128)S(1)} %bitcast_add_fusion.2, s32[]{:T(128)} %constant.246.clone.1..sunk, s32[]{:T(128)S(6)} %select_n.116, s32[]{:T(128)S(6)} %min.38) | dynamic-update-slice | bytes 1572868 | tf_op jit(solution)/shard_map/while/body/eval_jaxpr/dynamic_update_slice | solution.py:119
  528.6 11.0 %dynamic_update_slice.31 = f32[12,256,512]{2,1,0:T(8,128)} dynamic-update-slice(f32[12,256,512]{2,1,0:T(8,128)} %get-tuple-element.788, f32[12,128,128]{2,1,0:T(8,128)S(1)} %bitcast_add_fusion.2, s32[]{:T(128)} %constant.246.clone.1..sunk, s32[]{:T(128)S(6)} %select_n.116, s32[]{:T(128)S(6)} %min.38) | dynamic-update-slice | bytes 1572868 | tf_op jit(solution)/shard_map/while/body/eval_jaxpr/dynamic_update_slice | solution.py:119
  547.3 11.0 %dynamic_update_slice.31 = f32[12,256,512]{2,1,0:T(8,128)} dynamic-update-slice(f32[12,256,512]{2,1,0:T(8,128)} %get-tuple-element.788, f32[12,128,128]{2,1,0:T(8,128)S(1)} %bitcast_add_fusion.2, s32[]{:T(128)} %constant.246.clone.1..sunk, s32[]{:T(128)S(6)} %select_n.116, s32[]{:T(128)S(6)} %min.38) | dynamic-update-slice | bytes 1572868 | tf_op jit(solution)/shard_map/while/body/eval_jaxpr/dynamic_update_slice | solution.py:119
  563.7 10.1 %collective-permute-done.3 = bf16[1,128,256]{2,1,0:T(8,128)(2,1)S(1)} collective-permute-done((bf16[1,128,256]{2,1,0:T(8,128)(2,1)S(1)}, bf16[1,128,256]{2,1,0:T(8,128)(2,1)S(1)}, u32[]{:S(2)}, u32[]{:S(2)}) %collective-permute-start.3) | collective-permute-done | bytes 65568 | tf_op jit(solution)/shard_map/ppermute | solution.py:37
  573.9 2.8 add_divide_fusion
  (111 shorter events, 95.7 us)
Async XLA Ops:
  6.5 279.0 %all-gather.2.cloned.1.call-start = ((), (), s32[]{:S(2)}) async-start(), calls=%async_computation | async-start | bytes 7077888 | tf_op jit(solution)/shard_map/all_gather | solution.py:172
  39.9 5.8 collective-permute-start.1
  41.8 8.5 %collective-permute-start = (f32[12,16,256]{2,0,1:T(8,128)S(1)}, f32[12,16,256]{2,0,1:T(8,128)S(1)}, u32[]{:S(2)}, u32[]{:S(2)}) collective-permute-start(f32[12,16,256]{2,0,1:T(8,128)S(1)} %all_gather.6), channel_id=1, source_target_pairs={{0,8},{8,16},{16,24},{24,32},{32,40},{40,48},{48,56},{56,64},{64,7... | collective-permute-start | bytes 589832 | tf_op jit(solution)/shard_map/ppermute | solution.py:24
  58.3 230.7 %copy-start.1 = (s32[16,2]{0,1:T(2,128)S(1)}, s32[16,2]{0,1:T(2,128)}, u32[]{:S(2)}) copy-start(s32[16,2]{0,1:T(2,128)} %get-tuple-element.832) | copy-start | bytes 388
  58.3 230.7 %copy-start.8 = (s32[16]{0:T(128)S(1)}, s32[16]{0:T(128)}, u32[]{:S(2)}) copy-start(s32[16]{0:T(128)} %param.19) | copy-start | bytes 196
  559.8 14.0 %collective-permute-start.2 = (bf16[12,128,256]{2,1,0:T(8,128)(2,1)S(1)}, bf16[12,128,256]{2,1,0:T(8,128)(2,1)S(1)}, u32[]{:S(2)}, u32[]{:S(2)}) collective-permute-start(bf16[12,128,256]{2,1,0:T(8,128)(2,1)S(1)} %slice.49), channel_id=1, source_target_pairs={{0,8},{8,16},{16,24},{24,32},{32,40},{40,48},{48,56},{56,64},{64,7... | collective-permute-start | bytes 2359304 | tf_op jit(solution)/shard_map/ppermute | solution.py:37
  561.8 12.1 %collective-permute-start.3 = (bf16[1,128,256]{2,1,0:T(8,128)(2,1)S(1)}, bf16[1,128,256]{2,1,0:T(8,128)(2,1)S(1)}, u32[]{:S(2)}, u32[]{:S(2)}) collective-permute-start(bf16[1,128,256]{2,1,0:T(8,128)(2,1)S(1)} %slice.50), channel_id=1, source_target_pairs={{0,8},{8,16},{16,24},{24,32},{32,40},{40,48},{48,56},{56,64},{64,7... | collective-permute-start | bytes 196616 | tf_op jit(solution)/shard_map/ppermute | solution.py:37
Sparse Core Ops, SparseCore 0:
  58.4 227.0 all-gather.1
where the time goes:
time: 586 us; the launch traced here: 584 us
  waiting for transfers between devices  243 us (41%)
  local copies, waits for them, and re-layouts  208 us (35%)
  loops' own time  44 us (8%)
  other arithmetic  33.4 us (6%)
  blocking collectives  32.6 us (6%)
  between operations  13.5 us (2%)
  starting transfers between devices  8.16 us (1%)
    all_gather x1, waiting for transfers between devices, per_device(): lax.all_gather(part, 'patch', axis=0, tiled=True)  227 us
    dynamic_update_slice x16, local copies, waits for them, and re-layouts, place_patch(): lax.dynamic_update_slice(numerator, current + blend_scale * produced.asty...  150 us
    another operation x1, loops' own time, per_device(): numerator, cover = lax.fori_loop(0, piece.shape[0], absorb_one, empty_sums)  41.3 us
    all_gather x1, blocking collectives, per_device(): within = lax.all_gather(coarse_state, 'patch', axis=1, tiled=True)  32.6 us
    add x16, other arithmetic, place_patch(): current + blend_scale * produced.astype(jnp.float32)  28.9 us
    dynamic_update_slice x16, local copies, waits for them, and re-layouts, place_patch(): cover = lax.dynamic_update_slice(cover, covered + blend_scale, corner)  27.8 us
  transfers between devices with their start and end apart: 5, of which 4 were waited for; matrix products, arithmetic and copies ran while one was open for 0% of the time, Pallas kernels for 0%

commit v1 on v0

v1 whole, which is shorter than its diff:
```python
import math

import jax
import jax.numpy as jnp
from jax import lax
from jax.experimental import pallas as pl
from jax.experimental.pallas import tpu as pltpu
from jax.sharding import PartitionSpec as P

VARS = 12
CHAN = 128
PS = 128
F = 8
TH = 128
TW = 256
BF = jnp.bfloat16
F32 = jnp.float32
NT, NS = 8, 16
XR = (NT + 2) * NS
KC = 512
GROUP = PS * VARS


def dot(a, b):
    return jnp.dot(a, b, preferred_element_type=F32)


def dot_nt(a, b):
    return lax.dot_general(a, b, (((1,), (1,)), ((), ())), preferred_element_type=F32)


def split(x):
    hi = x.astype(BF)
    return hi, (x - hi.astype(F32)).astype(BF)


def row_halo(x):
    rows = x.shape[0]
    s = lax.broadcasted_iota(jnp.int32, (rows, NS, CHAN), 1)
    before = jnp.where(s == 0, 0.0, pltpu.roll(x[:, NT - 1], 1, 1))
    after = jnp.where(s == NS - 1, 0.0, pltpu.roll(x[:, 0], NS - 1, 1))
    return before, after


def interp_stage(hx, xpos, coarse, loc_ref, extra_ref, slot, xh, xl):
    chi, clo = split(coarse)
    t1 = dot_nt(hx, chi) + dot_nt(hx, clo) + xpos
    hi, lo = split(t1)
    lhs = jnp.concatenate([hi, lo], axis=0)
    v_at = lax.broadcasted_iota(jnp.int32, (16, 256), 0)
    ch_at = lax.broadcasted_iota(jnp.int32, (16, 256), 1) % 16
    diag = jnp.where((v_at == ch_at) & (v_at < VARS), 1.0, 0.0)

    def step(g, _):
        loc = jnp.broadcast_to(loc_ref[slot, g], (16, 256))
        blocks = []
        for c in range(28):
            hat = jnp.maximum(0.0, 1.0 - jnp.abs(loc - float(c))) * diag
            if c == 0:
                hat = hat + extra_ref[slot, g]
            blocks.append(hat.astype(BF))
        blocks.append(jnp.zeros((64, 256), BF))
        res = dot(lhs, jnp.concatenate(blocks, axis=0))
        x = res[:XR] + res[XR:]
        for h in range(2):
            xa, xb = split(x[:, h * 128 : h * 128 + 128])
            xh[2 * g + h] = xa.reshape(NT + 2, NS, 128)
            xl[2 * g + h] = xb.reshape(NT + 2, NS, 128)
        return 0

    lax.fori_loop(0, 16, step, 0)


def first_stage(win, b_in, xh, fa, shift, sums):
    bias = b_in[...]
    sums[...] = jnp.zeros_like(sums)

    def step(it, _):
        lhs = jnp.concatenate(
            [xh[pl.ds(4 * it, 4), dx : dx + 8].reshape(512, 128) for dx in range(3)], axis=1
        )
        acc = dot(lhs, win[...])
        parts = []
        for r in range(4):
            x = (acc[:, r * 128 : r * 128 + 128] + bias).astype(BF)
            for b in range(4):
                fa[8 * it + 2 * b + r // 2, r % 2] = x[b * 128 : b * 128 + 128]
            parts.append(x.astype(F32))

        @pl.when(it == 0)
        def _():
            shift[...] = jnp.mean(parts[0], axis=0, keepdims=True)

        base = shift[...]
        one = jnp.zeros((8, CHAN), F32)
        two = jnp.zeros((8, CHAN), F32)
        for x in parts:
            d = (x - base).reshape(64, 8, CHAN)
            one = one + jnp.sum(d, axis=0)
            two = two + jnp.sum(d * d, axis=0)
        sums[0] += one
        sums[1] += two
        return 0

    lax.fori_loop(0, 8, step, 0)


def group_mean(x):
    lane = lax.broadcasted_iota(jnp.int32, x.shape, 1)
    total = x
    for k in (1, 2):
        low = (lane // k) % 2 == 0
        total = total + jnp.where(low, pltpu.roll(total, CHAN - k, 1), pltpu.roll(total, k, 1))
    return total * 0.25


def scale_shift(sums, shift, gamma, beta):
    n = float(PS * PS)
    one = jnp.broadcast_to(jnp.sum(sums[0], axis=0, keepdims=True), (8, CHAN)) / n
    two = jnp.broadcast_to(jnp.sum(sums[1], axis=0, keepdims=True), (8, CHAN)) / n
    own_var = jnp.maximum(two - one * one, 0.0)
    mean = one + shift[...]
    g_mean = group_mean(mean)
    off = mean - g_mean
    g_var = group_mean(own_var + off * off)
    scale = gamma[...] / jnp.sqrt(g_var + 1e-05)
    return scale[0:1], (beta[...] - g_mean * scale)[0:1]


def norm_stage(scale, offset, fa, nb):
    half_scale = 0.5 * scale
    half_offset = 0.5 * offset

    def step(p, _):
        x = fa[p].astype(F32).reshape(2, NT, NS, CHAN)
        h = x * half_scale + half_offset
        y = h + h * jnp.tanh(h)
        before, after = row_halo(y)
        for r in range(2):
            at, k = (p, 1) if r == 0 else (p + 1, 0)
            nb[at, k, 1 : NT + 1] = y[r].astype(BF)
            nb[at, k, 0] = before[r].astype(BF)
            nb[at, k, NT + 1] = after[r].astype(BF)
        return 0

    lax.fori_loop(0, 64, step, 0, unroll=2)


def mid_stage(wmid, nb, fa, sb):
    def step(it, _):
        p0 = 4 * it
        lhs = []
        for k in range(4):
            for dx in range(3):
                lhs.append(nb[pl.ds(p0 + k // 2, 4), k % 2, dx : dx + 8].reshape(512, CHAN))
        acc = dot(jnp.concatenate(lhs, axis=1), wmid[...])
        for r in range(2):
            x = acc[:, r * 128 : r * 128 + 128] + fa[pl.ds(p0, 4), r].astype(F32).reshape(512, CHAN)
            x = x.reshape(4, NT, NS, CHAN)
            before, after = row_halo(x)
            for b in range(4):
                at = 2 * b + r + 1
                q, k = 2 * it + at // 4, at % 4
                sb[q, k, 1 : NT + 1] = x[b].astype(BF)
                sb[q, k, 0] = before[b].astype(BF)
                sb[q, k, NT + 1] = after[b].astype(BF)
        return 0

    lax.fori_loop(0, 16, step, 0)


def out_step(it, wout, sb, xh, xl):
    g0 = 4 * it
    lhs = [sb[pl.ds(g0 + k // 4, 4), k % 4].reshape(4 * XR, CHAN) for k in range(6)]
    lhs.append(xh[pl.ds(g0, 4)].reshape(4 * XR, CHAN))
    lhs.append(xl[pl.ds(g0, 4)].reshape(4 * XR, CHAN))
    acc = dot(jnp.concatenate(lhs, axis=1), wout[...])
    y0 = acc[:, :128].reshape(4, NT + 2, NS, 128)
    y1 = acc[:, 128:].reshape(4, NT + 2, NS, 128)
    centre = pltpu.roll(y0[:, 1 : NT + 1].reshape(512, 128), 64, 1).reshape(4, NT, NS, 128)
    res = y0[:, 0:NT] + centre + y1[:, 2 : NT + 2]
    res = res.reshape(4, 128, 128)
    lane = lax.broadcasted_iota(jnp.int32, (128, 128), 1)
    parts = []
    for h in range(2):
        both = jnp.where(lane < 48, res[2 * h], pltpu.roll(res[2 * h + 1], 48, 1))
        parts.append(jnp.transpose(both)[:96])
    return jnp.concatenate(parts, axis=0).astype(BF)


def patch_kernel(
    hx, xpos, loc, extra, coarse, win, b_in, gamma, beta, wmid, wout, out, xh, xl, fa, nb, sb, shift, sums
):
    zero = jnp.zeros((NT + 2, NS, CHAN), BF)
    nb[0, 0] = zero
    nb[64, 1] = zero
    sb[0, 0] = zero
    sb[32, 1] = zero

    def one_slot(slot, _):
        interp_stage(hx[slot], xpos[slot], coarse[...], loc, extra, slot, xh, xl)
        first_stage(win, b_in, xh, fa, shift, sums)
        scale, offset = scale_shift(sums, shift, gamma, beta)
        norm_stage(scale, offset, fa, nb)
        mid_stage(wmid, nb, fa, sb)

        def out_loop(it, _):
            at = pl.multiple_of(slot * GROUP + it * 192, 192)
            out[pl.ds(at, 192)] = out_step(it, wout, sb, xh, xl)
            return 0

        lax.fori_loop(0, 8, out_loop, 0)
        return 0

    lax.fori_loop(0, 2, one_slot, 0)


VM = pl.BlockSpec(memory_space=pltpu.VMEM)
SM = pl.BlockSpec(memory_space=pltpu.SMEM)


def run_patches(tables, coarse, weights):
    return pl.pallas_call(
        patch_kernel,
        out_shape=jax.ShapeDtypeStruct((2 * GROUP, 128), BF),
        in_specs=[VM] * 11,
        out_specs=VM,
        scratch_shapes=[
            pltpu.VMEM((32, NT + 2, NS, 128), BF),
            pltpu.VMEM((32, NT + 2, NS, 128), BF),
            pltpu.VMEM((64, 2, 128, CHAN), BF),
            pltpu.VMEM((65, 2, NT + 2, NS, CHAN), BF),
            pltpu.VMEM((33, 4, NT + 2, NS, CHAN), BF),
            pltpu.VMEM((1, CHAN), F32),
            pltpu.VMEM((2, 8, CHAN), F32),
        ],
        compiler_params=pltpu.CompilerParams(vmem_limit_bytes=56 * 2**20),
        name="patch_net",
    )(*tables, coarse, *weights)


def patch_tables(anchor_y, anchor_x, c0, height, breadth, limit_y, limit_x):
    rows = jnp.arange(XR)
    j = (rows % NS) * NT + rows // NS - 1
    good_x = (j >= 0) & (j < PS)
    x = (anchor_x[:, None] + j).astype(F32)
    at = jnp.clip((x + 0.5) / F - 0.5, 0.0, limit_x - 1.0)
    d = jnp.arange(limit_x).astype(F32)
    hx = jnp.maximum(0.0, 1.0 - jnp.abs(at[:, :, None] - d))
    hx = jnp.where(good_x[None, :, None], hx, 0.0).astype(BF)
    angle_x = x * (2.0 * math.pi / breadth)
    col = jnp.arange(KC)
    xpos = jnp.where(
        col == 12,
        1.0,
        jnp.where(
            col == 13,
            jnp.sin(angle_x)[:, :, None],
            jnp.where(col == 14, jnp.cos(angle_x)[:, :, None], 0.0),
        ),
    )
    xpos = jnp.where(good_x[None, :, None], xpos, 0.0).astype(F32)
    lane = jnp.arange(4096)
    b, k, ch = lane // 128, (lane % 128) // 16, lane % 16
    i = 4 * b - 1 + k
    good_y = (i >= 0) & (i < PS) & (k < 6)
    y = (anchor_y[:, None] + i).astype(F32)
    loc = jnp.clip((y + 0.5) / F - 0.5, 0.0, limit_y - 1.0) - c0.astype(F32)
    loc = jnp.where(good_y, loc, -1000.0).reshape(2, 16, 1, 256)
    angle_y = y * (2.0 * math.pi / height)
    ypos = jnp.where(ch == 12, jnp.sin(angle_y), jnp.where(ch == 13, jnp.cos(angle_y), 0.0))
    v = jnp.arange(16)[:, None]
    extra = jnp.where(v == 12, ypos[:, None], 0.0)
    extra = extra + jnp.where((v == 13) & (ch == 14) | (v == 14) & (ch == 15), 1.0, 0.0)
    extra = jnp.where(good_y, extra, 0.0).astype(F32)
    extra = extra.reshape(2, 16, 16, 256).transpose(0, 2, 1, 3)
    return hx, xpos, loc, extra


def packed_weights(w_in, b_in, gamma, beta, w_mid, w_out):
    w = w_in.transpose(1, 0, 2, 3)
    win = jnp.stack([jnp.pad(w, ((0, 0), (r, 5 - r), (0, 0), (0, 0))) for r in range(4)], axis=3)
    win = win.reshape(3 * 128, 4 * CHAN)
    wmid = jnp.stack([jnp.pad(w_mid, ((r, 1 - r), (0, 0), (0, 0), (0, 0))) for r in range(2)], axis=3)
    wmid = wmid.reshape(4 * 3 * CHAN, 2 * CHAN)
    wo = w_out.transpose(0, 2, 1, 3)
    wout = jnp.stack([jnp.pad(wo, ((r, 3 - r), (0, 0), (0, 0), (0, 0))) for r in range(4)], axis=3)
    wout = wout.reshape(6 * CHAN, 3, 48)
    wout = jnp.pad(wout, ((0, 0), (0, 1), (0, 16))).reshape(6 * CHAN, 256)
    row = jnp.arange(128)[:, None]
    colm = jnp.arange(256)[None]
    keep = (colm >= 64) & (colm < 112) & (row % 16 == (colm - 64) % 12) & (row // 16 == (colm - 64) // 12 + 1)
    ident = keep.astype(BF)
    wout = jnp.concatenate([wout, ident, ident], axis=0)
    return (
        win,
        b_in.reshape(1, CHAN),
        gamma.reshape(1, CHAN),
        beta.reshape(1, CHAN),
        wmid,
        wout,
    )


ACC_ROWS = (3 * TH // 2) * VARS


def place_kernel(info, gathered, num, over, acc, buf, sem):
    acc[...] = jnp.zeros_like(acc)
    lane = lax.broadcasted_iota(jnp.int32, (128, TW), 0)
    x_at = lax.broadcasted_iota(jnp.int32, (128, TW), 1)
    j_at = (lane % NS) * NT + lane // NS

    def fetch(s, k):
        return pltpu.make_async_copy(gathered.at[pl.ds(s * GROUP, GROUP)], buf.at[k], sem.at[k])

    fetch(0, 0).start()

    def slot(s, _):
        k = s % 2

        @pl.when(s < 15)
        def _():
            fetch(s + 1, 1 - k).start()

        fetch(s, k).wait()
        dy, dx, weight = info[0, s], info[1, s], info[2, s]

        @pl.when((weight > 0) & (dx > -PS) & (dx < TW))
        def _():
            onehot = jnp.where(x_at - j_at == dx, weight, 0).astype(F32).astype(BF)
            par = dy % 2
            base = ((dy - par) // 2) * 24

            def part(n, _):
                y = dot(buf[k, pl.ds(pl.multiple_of(n * 384, 384), 384)], onehot)
                at = pl.multiple_of(base + n * 384, 8)
                for h in range(2):
                    acc[par, h, pl.ds(at, 384)] += y[:, h * 128 : h * 128 + 128]
                return 0

            lax.fori_loop(0, 4, part, 0)

        return 0

    lax.fori_loop(0, 16, slot, 0)
    for v in range(VARS):
        for h in range(2):
            cols = slice(h * 128, h * 128 + 128)
            num[v, :, cols] = acc[0, h, pl.ds(v, TH, VARS)]
            num[v, 1:, cols] += acc[1, h, pl.ds(v, TH - 1, VARS)]
            low = acc[0, h, pl.ds(TH * VARS + v, TH // 2, VARS)]
            low = low + acc[1, h, pl.ds((TH - 1) * VARS + v, TH // 2, VARS)]
            over[v, :, cols] = low.astype(BF)


def run_place(info, gathered):
    return pl.pallas_call(
        place_kernel,
        out_shape=(
            jax.ShapeDtypeStruct((VARS, TH, TW), F32),
            jax.ShapeDtypeStruct((VARS, TH // 2, TW), BF),
        ),
        in_specs=[SM, pl.BlockSpec(memory_space=pl.ANY)],
        out_specs=(VM, VM),
        scratch_shapes=[
            pltpu.VMEM((2, 2, ACC_ROWS, 128), F32),
            pltpu.VMEM((2, GROUP, 128), BF),
            pltpu.SemaphoreType.DMA((2,)),
        ],
        compiler_params=pltpu.CompilerParams(vmem_limit_bytes=40 * 2**20),
        name="place",
    )(info, gathered)


def covered(dy, dx, weight, rows):
    r = jnp.arange(rows)
    c = jnp.arange(TW)
    in_r = (r >= dy[:, None]) & (r < dy[:, None] + PS)
    in_c = (c >= dx[:, None]) & (c < dx[:, None] + PS)
    left = jnp.where(in_r, weight[:, None], 0).astype(F32)
    return lax.dot_general(left, in_c.astype(F32), (((0,), (0,)), ((), ())), preferred_element_type=F32)


def per_device(coarse_state, anchors, region_count, blend, w_in, b_in, gamma, beta, w_mid, w_out):
    n_region = lax.axis_size("region")
    n_patch = lax.axis_size("patch")
    region = lax.axis_index("region")
    column = lax.axis_index("patch")
    limit = coarse_state.shape[1] * n_region * n_patch
    band = limit // n_region
    up = [(i, i + 1) for i in range(n_region - 1)]
    down = [(j, i) for i, j in up]

    slots = anchors.shape[0]
    weight = jnp.where(jnp.arange(slots) < region_count[0], blend, 0).astype(jnp.int32)
    dy = anchors[:, 0] - region * TH
    dx = anchors[:, 1] - column * TW
    info = jnp.stack([dy, dx, weight])
    above = lax.ppermute(jnp.stack([dy - TH, anchors[:, 1], weight]), "region", up)

    within = lax.all_gather(coarse_state.transpose(1, 0, 2), "patch", axis=0, tiled=True)
    before = lax.ppermute(within[band - 2 :], "region", up)
    after = lax.ppermute(within[:10], "region", down)
    coarse = jnp.concatenate([before, within, after], axis=0)
    coarse = jnp.pad(coarse, ((0, 4), (0, 4), (0, 0))).reshape(KC, limit)

    mine = lax.dynamic_slice(anchors, (column * 2, jnp.int32(0)), (2, 2))
    tables = patch_tables(
        mine[:, 0], mine[:, 1], region * band - 2, TH * n_region, TW * n_patch, limit, limit
    )
    weights = packed_weights(w_in, b_in, gamma, beta, w_mid, w_out)
    produced = run_patches(tables, coarse, weights)
    gathered = lax.all_gather(produced, "patch", axis=0, tiled=True)
    num, over = run_place(info, gathered)
    cover = covered(dy, dx, weight, TH) + covered(above[0], above[1] - column * TW, above[2], TH)
    low = lax.ppermute(over, "region", up).astype(F32)
    num = num + jnp.pad(low, ((0, 0), (0, TH // 2), (0, 0)))
    return num / jnp.maximum(cover, 1.0)


def solution(mesh):
    return jax.shard_map(
        per_device,
        mesh=mesh,
        in_specs=(
            P(None, ("region", "patch"), None),
            P("region", None),
            P("region"),
            P("region"),
            P(),
            P(),
            P(),
            P(),
            P(),
            P(),
        ),
        out_specs=P(None, "region", "patch"),
        check_vma=False,
    )
```

time: 586 us -> 237 us (0.40)
  the two profiles are of different devices: /device:TPU:104 before, /device:TPU:2 now
where the time goes in v1:
time: 237 us; the launch traced here: 235 us
  waiting for transfers between devices  94.8 us (40%)
  Pallas kernels  63.3 us (27%)
  blocking collectives  36 us (15%)
  between operations  14.4 us (6%)
  starting transfers between devices  9.39 us (4%)
  local copies, waits for them, and re-layouts  9.04 us (4%)
  other arithmetic  7.55 us (3%)
    all_gather x1, waiting for transfers between devices, per_device(): gathered = lax.all_gather(produced, 'patch', axis=0, tiled=True)  84.6 us
    pallas_call x1, Pallas kernels, run_patches(): pl.pallas_call(patch_kernel, out_shape=jax.ShapeDtypeStruct((2 * GROUP, 1...  57.8 us
    all_gather x1, blocking collectives, per_device(): lax.all_gather(coarse_state.transpose(1, 0, 2), 'patch', axis=0, tiled=True)  36 us
    ppermute x1, waiting for transfers between devices, per_device(): low = lax.ppermute(over, 'region', up).astype(F32)  7.78 us
    pallas_call x1, Pallas kernels, run_place(): pl.pallas_call(place_kernel, out_shape=(jax.ShapeDtypeStruct((VARS, TH, T...  5.52 us
    unnamed x13, local copies, waits for them, and re-layouts  5.36 us
  transfers between devices with their start and end apart: 5, of which 3 were waited for; matrix products, arithmetic and copies ran while one was open for 5% of the time, Pallas kernels for 0%

profile of v1, /device:TPU:2, one launch (start us, length us, event | category | flops | bytes accessed | tf_op | source)
XLA Modules:
  0.0 235.0 jit_solution(9312221976464621955)
XLA Ops:
  6.5 0.8 copy.31
  7.3 36.0 %all_gather.6 = f32[16,12,256]{2,1,0:T(8,128)S(1)} all-gather(f32[2,12,256]{2,1,0:T(8,128)S(1)} %bitcast.79), channel_id=1, replica_groups=mesh['region'=16,'patch'=8] {'patch'}, dimensions={0}, use_global_device_ids=true | all-gather | bytes 221184 | tf_op jit(solution)/shard_map/all_gather | solution.py:402
  43.3 1.9 collective-permute-start.1
  45.3 2.4 %collective-permute-start = (f32[2,12,256]{2,1,0:T(8,128)S(1)}, f32[2,12,256]{2,1,0:T(8,128)S(1)}, u32[]{:S(2)}, u32[]{:S(2)}) collective-permute-start(f32[2,12,256]{2,1,0:T(8,128)S(1)} %slice.40), channel_id=1, source_target_pairs={{0,8},{8,16},{16,24},{24,32},{32,40},{40,48},{48,56},{56,64},{64,7... | collective-permute-start | bytes 73736 | tf_op jit(solution)/shard_map/ppermute | solution.py:403
  47.9 0.8 constant_dynamic-slice_fusion
  48.7 1.1 pad_bitcast_fusion.1
  50.7 0.7 broadcast_select_fusion.loc
  51.9 0.8 pad_maximum_fusion.1.wout
  52.7 0.8 select_convert_fusion.hx
  53.6 1.0 add_select_fusion.extra
  54.6 1.0 select_select_fusion.xpos
  56.0 0.8 copy.30
  56.9 0.8 copy.21
  57.7 1.0 copy.29
  58.7 0.8 select_maximum_fusion
  59.5 57.8 %patch_net.1 = bf16[3072,128]{1,0:T(8,128)(2,1)} custom-call(bf16[2,160,256]{2,1,0:T(8,128)(2,1)} %select_convert_fusion.hx, f32[2,160,512]{2,1,0:T(8,128)} %select_select_fusion.xpos, f32[2,16,1,256]{3,2,1,0:T(1,128)} %broadcast_select_fusion.loc, f32[2,16,16,256]{3,2,1,0:T(8,128)} %add_select_fusion.extra, f32[512,256]{1,0:T(8,128)} %bitcast.75, ...), custom_call_target="tpu_custom_call" | custom-call | tf_op jit(solution)/shard_map/patch_net/pallas_call | solution.py:223
  118.0 3.1 %collective-permute-start.3 = (s32[3,16]{1,0:T(4,128)S(1)}, s32[3,16]{1,0:T(4,128)S(1)}, u32[]{:S(2)}, u32[]{:S(2)}) collective-permute-start(s32[3,16]{1,0:T(4,128)S(1)} %get-tuple-element.35), channel_id=1, source_target_pairs={{0,8},{8,16},{16,24},{24,32},{32,40},{40,48},{48,56},{56,64},{64,7... | collective-permute-start | bytes 584 | tf_op jit(solution)/shard_map/ppermute | solution.py:400
  121.5 2.4 %collective-permute-done.3 = s32[3,16]{1,0:T(4,128)S(1)} collective-permute-done((s32[3,16]{1,0:T(4,128)S(1)}, s32[3,16]{1,0:T(4,128)S(1)}, u32[]{:S(2)}, u32[]{:S(2)}) %collective-permute-start.3) | collective-permute-done | bytes 224 | tf_op jit(solution)/shard_map/ppermute | solution.py:400
  123.8 84.6 %all-gather.2.cloned.1.call-done.gathered = bf16[24576,128]{1,0:T(8,128)(2,1)} async-done(((bf16[3072,128]{1,0:T(8,128)(2,1)}), bf16[24576,128]{1,0:T(8,128)(2,1)}) %all-gather.2.cloned.1.call-update) | async-done | bytes 6291472 | tf_op jit(solution)/shard_map/all_gather | solution.py:414
  208.5 2.8 %copy-done = bf16[24576,128]{1,0:T(8,128)(2,1)S(1)} copy-done((bf16[24576,128]{1,0:T(8,128)(2,1)S(1)}, bf16[24576,128]{1,0:T(8,128)(2,1)}, u32[]{:S(2)}) %copy-start) | copy-done | bytes 6291480
  211.2 5.5 %place.1 = (f32[12,128,256]{2,1,0:T(8,128)S(1)}, bf16[12,64,256]{2,1,0:T(8,128)(2,1)S(1)}) custom-call(s32[3,16]{1,0:T(4,128)S(1)} %get-tuple-element.36.info, bf16[24576,128]{1,0:T(8,128)(2,1)S(1)} %copy-done), custom_call_target="tpu_custom_call" | custom-call | tf_op jit(solution)/shard_map/place/pallas_call | solution.py:358
  216.8 1.9 collective-permute-start.2
  219.0 7.8 %collective-permute-done.2 = bf16[12,64,256]{2,1,0:T(8,128)(2,1)S(1)} collective-permute-done((bf16[12,64,256]{2,1,0:T(8,128)(2,1)S(1)}, bf16[12,64,256]{2,1,0:T(8,128)(2,1)S(1)}, u32[]{:S(2)}, u32[]{:S(2)}) %collective-permute-start.2) | collective-permute-done | bytes 393248 | tf_op jit(solution)/shard_map/ppermute | solution.py:417
  226.8 1.4 add_divide_fusion
  (54 shorter events, 2.5 us)
Async XLA Ops:
  6.5 43.3 %copy-start.1 = (bf16[3,3,128,12]{2,3,1,0:T(8,128)(2,1)S(1)}, bf16[3,3,128,12]{2,3,1,0:T(8,128)(2,1)}, u32[]{:S(2)}) copy-start(bf16[3,3,128,12]{2,3,1,0:T(8,128)(2,1)} %param.19) | copy-start | bytes 82948
  6.5 201.9 %all-gather.2.cloned.1.call-start = ((), (), s32[]{:S(2)}) async-start(), calls=%async_computation | async-start | bytes 7077888 | tf_op jit(solution)/shard_map/all_gather | solution.py:414
  43.3 15.3 %collective-permute-start.1 = (f32[10,12,256]{2,1,0:T(8,128)S(1)}, f32[10,12,256]{2,1,0:T(8,128)S(1)}, u32[]{:S(2)}, u32[]{:S(2)}) collective-permute-start(f32[10,12,256]{2,1,0:T(8,128)S(1)} %slice.41), channel_id=1, source_target_pairs={{8,0},{16,8},{24,16},{32,24},{40,32},{48,40},{56,48},{64,56},{72,6... | collective-permute-start | bytes 368648 | tf_op jit(solution)/shard_map/ppermute | solution.py:404
  45.3 13.4 %collective-permute-start = (f32[2,12,256]{2,1,0:T(8,128)S(1)}, f32[2,12,256]{2,1,0:T(8,128)S(1)}, u32[]{:S(2)}, u32[]{:S(2)}) collective-permute-start(f32[2,12,256]{2,1,0:T(8,128)S(1)} %slice.40), channel_id=1, source_target_pairs={{0,8},{8,16},{16,24},{24,32},{32,40},{40,48},{48,56},{56,64},{64,7... | collective-permute-start | bytes 73736 | tf_op jit(solution)/shard_map/ppermute | solution.py:403
  51.7 3.9 %copy-start.2 = (bf16[3,3,16,128]{3,2,1,0:T(8,128)(2,1)S(1)}, bf16[3,3,16,128]{3,2,1,0:T(8,128)(2,1)}, u32[]{:S(2)}) copy-start(bf16[3,3,16,128]{3,2,1,0:T(8,128)(2,1)} %param.14) | copy-start | bytes 110596
  59.5 58.4 %copy-start.4 = (s32[16]{0:T(128)S(1)}, s32[16]{0:T(128)}, u32[]{:S(2)}) copy-start(s32[16]{0:T(128)} %param.13) | copy-start | bytes 196
  59.5 58.5 %copy-start.3 = (s32[16,2]{0,1:T(2,128)S(1)}, s32[16,2]{0,1:T(2,128)}, u32[]{:S(2)}) copy-start(s32[16,2]{0,1:T(2,128)} %param.11) | copy-start | bytes 388
  118.0 5.8 %collective-permute-start.3 = (s32[3,16]{1,0:T(4,128)S(1)}, s32[3,16]{1,0:T(4,128)S(1)}, u32[]{:S(2)}, u32[]{:S(2)}) collective-permute-start(s32[3,16]{1,0:T(4,128)S(1)} %get-tuple-element.35), channel_id=1, source_target_pairs={{0,8},{8,16},{16,24},{24,32},{32,40},{40,48},{48,56},{56,64},{64,7... | collective-permute-start | bytes 584 | tf_op jit(solution)/shard_map/ppermute | solution.py:400
  208.5 2.8 %copy-start = (bf16[24576,128]{1,0:T(8,128)(2,1)S(1)}, bf16[24576,128]{1,0:T(8,128)(2,1)}, u32[]{:S(2)}) copy-start(bf16[24576,128]{1,0:T(8,128)(2,1)} %all-gather.2.cloned.1.call-done.gathered) | copy-start | bytes 18874372
  216.8 10.0 %collective-permute-start.2 = (bf16[12,64,256]{2,1,0:T(8,128)(2,1)S(1)}, bf16[12,64,256]{2,1,0:T(8,128)(2,1)S(1)}, u32[]{:S(2)}, u32[]{:S(2)}) collective-permute-start(bf16[12,64,256]{2,1,0:T(8,128)(2,1)S(1)} %get-tuple-element.8), channel_id=1, source_target_pairs={{0,8},{8,16},{16,24},{24,32},{32,40},{40,48},{48,56},{56,64},{64,7... | collective-permute-start | bytes 1179656 | tf_op jit(solution)/shard_map/ppermute | solution.py:417
Sparse Core Ops, SparseCore 0:
  117.4 90.9 all-gather.1

commit v2 on v1

--- a/solution.py
+++ b/solution.py
@@ -19,6 +19,7 @@
 XR = (NT + 2) * NS
 KC = 512
 GROUP = PS * VARS
+MESH = pl.DeviceIdType.MESH
 
 
 def dot(a, b):
@@ -71,7 +72,7 @@
     lax.fori_loop(0, 16, step, 0)
 
 
-def first_stage(win, b_in, xh, fa, shift, sums):
+def first_stage(win, b_in, xh, fa, shift, sums, also):
     bias = b_in[...]
     sums[...] = jnp.zeros_like(sums)
 
@@ -100,6 +101,7 @@
             two = two + jnp.sum(d * d, axis=0)
         sums[0] += one
         sums[1] += two
+        also(it)
         return 0
 
     lax.fori_loop(0, 8, step, 0)
@@ -146,27 +148,23 @@
     lax.fori_loop(0, 64, step, 0, unroll=2)
 
 
-def mid_stage(wmid, nb, fa, sb):
-    def step(it, _):
-        p0 = 4 * it
-        lhs = []
-        for k in range(4):
-            for dx in range(3):
-                lhs.append(nb[pl.ds(p0 + k // 2, 4), k % 2, dx : dx + 8].reshape(512, CHAN))
-        acc = dot(jnp.concatenate(lhs, axis=1), wmid[...])
-        for r in range(2):
-            x = acc[:, r * 128 : r * 128 + 128] + fa[pl.ds(p0, 4), r].astype(F32).reshape(512, CHAN)
-            x = x.reshape(4, NT, NS, CHAN)
-            before, after = row_halo(x)
-            for b in range(4):
-                at = 2 * b + r + 1
-                q, k = 2 * it + at // 4, at % 4
-                sb[q, k, 1 : NT + 1] = x[b].astype(BF)
-                sb[q, k, 0] = before[b].astype(BF)
-                sb[q, k, NT + 1] = after[b].astype(BF)
-        return 0
-
-    lax.fori_loop(0, 16, step, 0)
+def mid_step(it, wmid, nb, fa, sb):
+    p0 = 4 * it
+    lhs = []
+    for k in range(4):
+        for dx in range(3):
+            lhs.append(nb[pl.ds(p0 + k // 2, 4), k % 2, dx : dx + 8].reshape(512, CHAN))
+    acc = dot(jnp.concatenate(lhs, axis=1), wmid[...])
+    for r in range(2):
+        x = acc[:, r * 128 : r * 128 + 128] + fa[pl.ds(p0, 4), r].astype(F32).reshape(512, CHAN)
+        x = x.reshape(4, NT, NS, CHAN)
+        before, after = row_halo(x)
+        for b in range(4):
+            at = 2 * b + r + 1
+            q, k = 2 * it + at // 4, at % 4
+            sb[q, k, 1 : NT + 1] = x[b].astype(BF)
+            sb[q, k, 0] = before[b].astype(BF)
+            sb[q, k, NT + 1] = after[b].astype(BF)
 
 
 def out_step(it, wout, sb, xh, xl):
@@ -188,9 +186,195 @@
     return jnp.concatenate(parts, axis=0).astype(BF)
 
 
+def exchange_kernel(shard, out, send_sem, recv_sem):
+    r, p = lax.axis_index("region"), lax.axis_index("patch")
+    n_r, n_p = lax.axis_size("region"), lax.axis_size("patch")
+    has_up, has_down = r > 0, r < n_r - 1
+    barrier = pltpu.get_barrier_semaphore()
+
+    out[28:32] = jnp.zeros((4, 16, 256), F32)
+
+    @pl.when(r == 0)
+    def _():
+        out[0:2] = jnp.zeros((2, 16, 256), F32)
+
+    @pl.when(r == n_r - 1)
+    def _():
+        out[18:28] = jnp.zeros((10, 16, 256), F32)
+
+    out[pl.ds(2 + 2 * p, 2)] = shard[...]
+
+    def greet(to):
+        pl.semaphore_signal(barrier, inc=1, device_id=to, device_id_type=MESH)
+
+    for d in range(1, n_p):
+        greet((r, (p + d) % n_p))
+
+    @pl.when(has_up)
+    def _():
+        greet((r - 1, n_p - 1))
+
+    @pl.when(has_down)
+    def _():
+        for k in range(5):
+            greet((r + 1, k))
+
+    feeds_down = (p == n_p - 1) & has_down
+    feeds_up = (p < 5) & has_up
+    count = n_p - 1 + jnp.where(feeds_down, n_p, 0) + jnp.where(feeds_up, n_p, 0)
+    pl.semaphore_wait(barrier, count)
+
+    def copy(row, key, k, to):
+        return pltpu.make_async_remote_copy(
+            src_ref=shard,
+            dst_ref=out.at[pl.ds(row, 2)],
+            send_sem=send_sem.at[k],
+            recv_sem=recv_sem.at[key],
+            device_id=to,
+            device_id_type=MESH,
+        )
+
+    def to_down(k):
+        return copy(0, 0, 7 + k, (r + 1, k))
+
+    def to_up(k):
+        return copy(18 + 2 * p, 9 + p, 15 + k, (r - 1, k))
+
+    def to_peer(d):
+        return copy(2 + 2 * p, 1 + p, d - 1, (r, (p + d) % n_p))
+
+    def each(act):
+        @pl.when(feeds_down)
+        def _():
+            for k in range(n_p):
+                act(to_down(k))
+
+        @pl.when(feeds_up)
+        def _():
+            for k in range(n_p):
+                act(to_up(k))
+
+        for d in range(1, n_p):
+            act(to_peer(d))
+
+    each(lambda c: c.start())
+
+    for d in range(1, n_p):
+        q = (p + d) % n_p
+        copy(2 + 2 * q, 1 + q, 0, (r, q)).wait_recv()
+
+    @pl.when(has_up)
+    def _():
+        copy(0, 0, 0, (r - 1, 7)).wait_recv()
+
+    @pl.when(has_down)
+    def _():
+        for k in range(5):
+            copy(18 + 2 * k, 9 + k, 0, (r + 1, k)).wait_recv()
+
+    each(lambda c: c.wait_send())
+
+
+def run_exchange(shard):
+    return pl.pallas_call(
+        exchange_kernel,
+        out_shape=jax.ShapeDtypeStruct((32, 16, 256), F32),
+        in_specs=[VM],
+        out_specs=VM,
+        scratch_shapes=[pltpu.SemaphoreType.DMA((23,)), pltpu.SemaphoreType.DMA((14,))],
+        compiler_params=pltpu.CompilerParams(collective_id=0, has_side_effects=True),
+        name="coarse_rows",
+    )(shard)
+
+
+CHUNK = 16 * VARS
+HALF = CHUNK // 2
+
+
+class Sharer:
+    def __init__(self, out, g, send_sem, recv_sem, tail_sem, own_sem):
+        self.out, self.g = out, g
+        self.send_sem, self.recv_sem = send_sem, recv_sem
+        self.tail_sem, self.own_sem = tail_sem, own_sem
+        p = lax.axis_index("patch")
+        z, y = p // 2, p % 2
+        self.me = p
+        self.fore = ((z + 1) % 4) * 2 + y
+        self.back = ((z + 3) % 4) * 2 + y
+        self.pair = z * 2 + 1 - y
+        self.fore_pair = ((z + 1) % 4) * 2 + 1 - y
+        self.back_pair = ((z + 3) % 4) * 2 + 1 - y
+
+    def at(self, owner, q, half=None):
+        start = (owner * 16 + q) * CHUNK
+        if half is None:
+            return self.g.at[pl.ds(pl.multiple_of(start, CHUNK), CHUNK)]
+        return self.g.at[pl.ds(pl.multiple_of(start + half * HALF, HALF), HALF)]
+
+    def remote(self, src, dst, stream, sem, to):
+        return pltpu.make_async_remote_copy(
+            src_ref=src,
+            dst_ref=dst,
+            send_sem=self.send_sem.at[stream],
+            recv_sem=sem,
+            device_id={"patch": to},
+            device_id_type=MESH,
+        )
+
+    def greet(self):
+        barrier = pltpu.get_barrier_semaphore()
+        for to in (self.fore, self.back, self.pair):
+            pl.semaphore_signal(barrier, inc=1, device_id={"patch": to}, device_id_type=MESH)
+        pl.semaphore_wait(barrier, 3)
+
+    def arrived(self, owner, q, stream):
+        there = self.at(owner, q)
+        self.remote(there, there, stream, self.recv_sem.at[stream, q], self.fore).wait_recv()
+
+    def own(self, q):
+        src = self.out.at[pl.ds(pl.multiple_of(q * CHUNK, CHUNK), CHUNK)]
+        dst = self.at(self.me, q)
+        self.remote(src, dst, 2, self.recv_sem.at[2, q], self.pair).start()
+        self.remote(src, dst, 0, self.recv_sem.at[0, q], self.fore).start()
+        self.remote(src, dst, 1, self.recv_sem.at[1, q], self.back).start()
+        pltpu.make_async_copy(src, dst, self.own_sem).start()
+
+    def first(self, q):
+        self.arrived(self.pair, q, 2)
+        there = self.at(self.pair, q)
+        self.remote(there, there, 3, self.recv_sem.at[3, q], self.fore).start()
+        self.remote(there, there, 4, self.recv_sem.at[4, q], self.back).start()
+        self.arrived(self.back, q, 0)
+        there = self.at(self.back, q, 0)
+        self.remote(there, there, 5, self.tail_sem.at[0], self.fore).start()
+        self.arrived(self.fore, q, 1)
+        there = self.at(self.fore, q, 1)
+        self.remote(there, there, 6, self.tail_sem.at[1], self.back).start()
+
+    def second(self, q):
+        self.arrived(self.back_pair, q, 3)
+        there = self.at(self.back_pair, q, 0)
+        self.remote(there, there, 7, self.tail_sem.at[2], self.fore).start()
+        self.arrived(self.fore_pair, q, 4)
+        there = self.at(self.fore_pair, q, 1)
+        self.remote(there, there, 8, self.tail_sem.at[3], self.back).start()
+
+    def finish(self):
+        whole = self.g.at[pl.ds(0, 2 * GROUP)]
+        part = self.g.at[pl.ds(0, GROUP)]
+        for k in range(4):
+            self.remote(part, part, 5 + k, self.tail_sem.at[k], self.fore).wait()
+        for k in range(5):
+            self.remote(whole, whole, k, self.tail_sem.at[0], self.fore).wait_send()
+        pltpu.make_async_copy(whole, whole, self.own_sem).wait()
+
+
 def patch_kernel(
-    hx, xpos, loc, extra, coarse, win, b_in, gamma, beta, wmid, wout, out, xh, xl, fa, nb, sb, shift, sums
+    hx, xpos, loc, extra, coarse, win, b_in, gamma, beta, wmid, wout, g,
+    out, xh, xl, fa, nb, sb, shift, sums, send_sem, recv_sem, tail_sem, own_sem,
 ):
+    share = Sharer(out, g, send_sem, recv_sem, tail_sem, own_sem)
+    share.greet()
     zero = jnp.zeros((NT + 2, NS, CHAN), BF)
     nb[0, 0] = zero
     nb[64, 1] = zero
@@ -199,20 +383,59 @@
 
     def one_slot(slot, _):
         interp_stage(hx[slot], xpos[slot], coarse[...], loc, extra, slot, xh, xl)
-        first_stage(win, b_in, xh, fa, shift, sums)
+
+        def forward(it):
+            @pl.when(slot == 1)
+            def _():
+                share.first(it)
+
+        first_stage(win, b_in, xh, fa, shift, sums, forward)
         scale, offset = scale_shift(sums, shift, gamma, beta)
         norm_stage(scale, offset, fa, nb)
-        mid_stage(wmid, nb, fa, sb)
-
-        def out_loop(it, _):
-            at = pl.multiple_of(slot * GROUP + it * 192, 192)
-            out[pl.ds(at, 192)] = out_step(it, wout, sb, xh, xl)
+
+        def out_chunk(it):
+            q = slot * 8 + it
+            at = pl.multiple_of(q * CHUNK, CHUNK)
+            out[pl.ds(at, CHUNK)] = out_step(it, wout, sb, xh, xl)
+            share.own(q)
+
+        def rows(it, _):
+            mid_step(2 * it, wmid, nb, fa, sb)
+            mid_step(2 * it + 1, wmid, nb, fa, sb)
+
+            @pl.when(it > 0)
+            def _():
+                out_chunk(it - 1)
+
+            @pl.when(slot == 1)
+            def _():
+                share.second(it)
+
+                @pl.when(it >= 3)
+                def _():
+                    share.first(8 + it - 3)
+
+                @pl.when(it >= 5)
+                def _():
+                    share.second(8 + it - 5)
+
             return 0
 
-        lax.fori_loop(0, 8, out_loop, 0)
+        lax.fori_loop(0, 8, rows, 0)
+        out_chunk(7)
         return 0
 
     lax.fori_loop(0, 2, one_slot, 0)
+
+    def drain(n, _):
+        share.first(13 + n)
+        share.second(11 + n)
+        return 0
+
+    lax.fori_loop(0, 3, drain, 0)
+    share.second(14)
+    share.second(15)
+    share.finish()
 
 
 VM = pl.BlockSpec(memory_space=pltpu.VMEM)
@@ -222,10 +445,11 @@
 def run_patches(tables, coarse, weights):
     return pl.pallas_call(
         patch_kernel,
-        out_shape=jax.ShapeDtypeStruct((2 * GROUP, 128), BF),
+        out_shape=jax.ShapeDtypeStruct((16 * GROUP, 128), BF),
         in_specs=[VM] * 11,
-        out_specs=VM,
+        out_specs=pl.BlockSpec(memory_space=pltpu.HBM),
         scratch_shapes=[
+            pltpu.VMEM((2 * GROUP, 128), BF),
             pltpu.VMEM((32, NT + 2, NS, 128), BF),
             pltpu.VMEM((32, NT + 2, NS, 128), BF),
             pltpu.VMEM((64, 2, 128, CHAN), BF),
@@ -233,8 +457,14 @@
             pltpu.VMEM((33, 4, NT + 2, NS, CHAN), BF),
             pltpu.VMEM((1, CHAN), F32),
             pltpu.VMEM((2, 8, CHAN), F32),
+            pltpu.SemaphoreType.DMA((9,)),
+            pltpu.SemaphoreType.DMA((5, 16)),
+            pltpu.SemaphoreType.DMA((4,)),
+            pltpu.SemaphoreType.DMA,
         ],
-        compiler_params=pltpu.CompilerParams(vmem_limit_bytes=56 * 2**20),
+        compiler_params=pltpu.CompilerParams(
+            vmem_limit_bytes=56 * 2**20, collective_id=1, has_side_effects=True
+        ),
         name="patch_net",
     )(*tables, coarse, *weights)
 
@@ -361,7 +591,7 @@
             jax.ShapeDtypeStruct((VARS, TH, TW), F32),
             jax.ShapeDtypeStruct((VARS, TH // 2, TW), BF),
         ),
-        in_specs=[SM, pl.BlockSpec(memory_space=pl.ANY)],
+        in_specs=[SM, pl.BlockSpec(memory_space=pltpu.HBM)],
         out_specs=(VM, VM),
         scratch_shapes=[
             pltpu.VMEM((2, 2, ACC_ROWS, 128), F32),
@@ -390,7 +620,6 @@
     limit = coarse_state.shape[1] * n_region * n_patch
     band = limit // n_region
     up = [(i, i + 1) for i in range(n_region - 1)]
-    down = [(j, i) for i, j in up]
 
     slots = anchors.shape[0]
     weight = jnp.where(jnp.arange(slots) < region_count[0], blend, 0).astype(jnp.int32)
@@ -399,19 +628,15 @@
     info = jnp.stack([dy, dx, weight])
     above = lax.ppermute(jnp.stack([dy - TH, anchors[:, 1], weight]), "region", up)
 
-    within = lax.all_gather(coarse_state.transpose(1, 0, 2), "patch", axis=0, tiled=True)
-    before = lax.ppermute(within[band - 2 :], "region", up)
-    after = lax.ppermute(within[:10], "region", down)
-    coarse = jnp.concatenate([before, within, after], axis=0)
-    coarse = jnp.pad(coarse, ((0, 4), (0, 4), (0, 0))).reshape(KC, limit)
+    shard = jnp.pad(coarse_state.transpose(1, 0, 2), ((0, 0), (0, 4), (0, 0)))
+    coarse = run_exchange(shard).reshape(KC, limit)
 
     mine = lax.dynamic_slice(anchors, (column * 2, jnp.int32(0)), (2, 2))
     tables = patch_tables(
         mine[:, 0], mine[:, 1], region * band - 2, TH * n_region, TW * n_patch, limit, limit
     )
     weights = packed_weights(w_in, b_in, gamma, beta, w_mid, w_out)
-    produced = run_patches(tables, coarse, weights)
-    gathered = lax.all_gather(produced, "patch", axis=0, tiled=True)
+    gathered = run_patches(tables, coarse, weights)
     num, over = run_place(info, gathered)
     cover = covered(dy, dx, weight, TH) + covered(above[0], above[1] - column * TW, above[2], TH)
     low = lax.ppermute(over, "region", up).astype(F32)

time: 237 us -> 140 us (0.59)
  waiting for transfers between devices: 94.8 us -> 7.46 us
  Pallas kernels: 63.3 us -> 106 us
  blocking collectives: 36 us -> 0 us
  between operations: 14.4 us -> 0.94 us
  starting transfers between devices: 9.39 us -> 3.84 us
    all_gather x1 -> x0, waiting for transfers between devices: 84.6 us -> none  [per_device(): gathered = lax.all_gather(produced, 'patch', axis=0, tiled=True)]
    pallas_call x1 -> x2, Pallas kernels: 57.8 us -> 101 us  [the longest x1 83.8 us: run_patches(): pl.pallas_call(patch_kernel, out_shape=jax.ShapeDtypeStruct((16 * GROUP,...]
    all_gather x1 -> x0, blocking collectives: 36 us -> none  [per_device(): lax.all_gather(coarse_state.transpose(1, 0, 2), 'patch', axis=0, tiled=True)]
    ppermute x2 -> x0, starting transfers between devices: 4.33 us -> none  [the longest x1 2.41 us: per_device(): before = lax.ppermute(within[band - 2:], 'region', up)]
    unnamed x13 -> x11, local copies, waits for them, and re-layouts: 5.36 us -> 5.38 us
  transfers between devices with their start and end apart: 5 -> 2, of which waited for: 3 -> 1; matrix products, arithmetic and copies ran while one was open for 5% -> 9% of each run, Pallas kernels for 0% -> 77%
where the time goes in v2:
time: 140 us; the launch traced here: 137 us
  Pallas kernels  106 us (76%)
  local copies, waits for them, and re-layouts  9.6 us (7%)
  other arithmetic  8.85 us (6%)
  waiting for transfers between devices  7.46 us (5%)
  starting transfers between devices  3.84 us (3%)
    pallas_call x1, Pallas kernels, run_patches(): pl.pallas_call(patch_kernel, out_shape=jax.ShapeDtypeStruct((16 * GROUP,...  83.8 us
    pallas_call x1, Pallas kernels, run_exchange(): pl.pallas_call(exchange_kernel, out_shape=jax.ShapeDtypeStruct((32, 16, 2...  16.9 us
    ppermute x1, waiting for transfers between devices, per_device(): low = lax.ppermute(over, 'region', up).astype(F32)  7.46 us
    pallas_call x1, Pallas kernels, run_place(): pl.pallas_call(place_kernel, out_shape=(jax.ShapeDtypeStruct((VARS, TH, T...  5.52 us
    unnamed x11, local copies, waits for them, and re-layouts  5.38 us
  transfers between devices with their start and end apart: 2, of which 1 were waited for; matrix products, arithmetic and copies ran while one was open for 9% of the time, Pallas kernels for 77%

profile of v2, /device:TPU:2, one launch (start us, length us, event | category | flops | bytes accessed | tf_op | source)
XLA Modules:
  0.0 137.5 jit_solution(9571054961839231503)
XLA Ops:
  0.7 0.7 slice_bitcast_fusion.4
  1.3 0.8 broadcast_add_fusion.2
  2.1 0.7 fusion.57
  2.8 1.9 %collective-permute-start.1 = (s32[3,16]{1,0:T(4,128)S(1)}, s32[3,16]{1,0:T(4,128)S(1)}, u32[]{:S(2)}, u32[]{:S(2)}) collective-permute-start(s32[3,16]{1,0:T(4,128)S(1)} %get-tuple-element.35), channel_id=1, source_target_pairs={{0,8},{8,16},{16,24},{24,32},{32,40},{40,48},{48,56},{56,64},{64,7... | collective-permute-start | bytes 584 | tf_op jit(solution)/shard_map/ppermute | solution.py:629
  5.0 0.8 constant_dynamic-slice_fusion
  5.7 0.7 copy.26
  6.5 0.6 pad.55.shard
  7.1 16.9 %coarse_rows.1 = f32[32,16,256]{2,1,0:T(8,128)} custom-call(f32[2,16,256]{2,1,0:T(8,128)} %pad.55.shard), custom_call_target="tpu_custom_call" | custom-call | tf_op jit(solution)/shard_map/coarse_rows/pallas_call | solution.py:279
  24.0 1.0 pad_bitcast_fusion.5
  25.0 0.3 copy.15
  25.3 0.9 copy.25
  26.5 0.8 copy.16
  27.3 1.0 copy.24
  29.1 0.8 broadcast_select_fusion.loc
  30.2 0.9 pad_maximum_fusion.1.wout
  31.1 0.8 select_convert_fusion.hx
  32.0 0.9 add_select_fusion.extra
  32.9 1.0 select_select_fusion.xpos
  34.0 83.8 %patch_net.1.gathered = bf16[24576,128]{1,0:T(8,128)(2,1)} custom-call(bf16[2,160,256]{2,1,0:T(8,128)(2,1)} %select_convert_fusion.hx, f32[2,160,512]{2,1,0:T(8,128)} %select_select_fusion.xpos, f32[2,16,1,256]{3,2,1,0:T(1,128)} %broadcast_select_fusion.loc, f32[2,16,16,256]{3,2,1,0:T(8,128)} %add_select_fusion.extra, f32[512,256]{1,0:T(8,128)} %bitcast.75, ...), custom_call_target="tpu_custom_call" | custom-call | tf_op jit(solution)/shard_map/patch_net/pallas_call | solution.py:446
  117.8 2.8 %copy-done = bf16[24576,128]{1,0:T(8,128)(2,1)S(1)} copy-done((bf16[24576,128]{1,0:T(8,128)(2,1)S(1)}, bf16[24576,128]{1,0:T(8,128)(2,1)}, u32[]{:S(2)}) %copy-start) | copy-done | bytes 6291480
  120.6 5.5 %place.1 = (f32[12,128,256]{2,1,0:T(8,128)S(1)}, bf16[12,64,256]{2,1,0:T(8,128)(2,1)S(1)}) custom-call(s32[3,16]{1,0:T(4,128)S(1)} %get-tuple-element.36.info, bf16[24576,128]{1,0:T(8,128)(2,1)S(1)} %copy-done), custom_call_target="tpu_custom_call" | custom-call | tf_op jit(solution)/shard_map/place/pallas_call | solution.py:588
  126.1 1.9 %collective-permute-start = (bf16[12,64,256]{2,1,0:T(8,128)(2,1)S(1)}, bf16[12,64,256]{2,1,0:T(8,128)(2,1)S(1)}, u32[]{:S(2)}, u32[]{:S(2)}) collective-permute-start(bf16[12,64,256]{2,1,0:T(8,128)(2,1)S(1)} %get-tuple-element.8), channel_id=1, source_target_pairs={{0,8},{8,16},{16,24},{24,32},{32,40},{40,48},{48,56},{56,64},{64,7... | collective-permute-start | bytes 1179656 | tf_op jit(solution)/shard_map/ppermute | solution.py:642
  128.7 7.5 %collective-permute-done = bf16[12,64,256]{2,1,0:T(8,128)(2,1)S(1)} collective-permute-done((bf16[12,64,256]{2,1,0:T(8,128)(2,1)S(1)}, bf16[12,64,256]{2,1,0:T(8,128)(2,1)S(1)}, u32[]{:S(2)}, u32[]{:S(2)}) %collective-permute-start) | collective-permute-done | bytes 393248 | tf_op jit(solution)/shard_map/ppermute | solution.py:642
  136.1 1.4 add_divide_fusion
  (43 shorter events, 2.3 us)
Async XLA Ops:
  2.8 125.6 %collective-permute-start.1 = (s32[3,16]{1,0:T(4,128)S(1)}, s32[3,16]{1,0:T(4,128)S(1)}, u32[]{:S(2)}, u32[]{:S(2)}) collective-permute-start(s32[3,16]{1,0:T(4,128)S(1)} %get-tuple-element.35), channel_id=1, source_target_pairs={{0,8},{8,16},{16,24},{24,32},{32,40},{40,48},{48,56},{56,64},{64,7... | collective-permute-start | bytes 584 | tf_op jit(solution)/shard_map/ppermute | solution.py:629
  7.1 19.1 %copy-start.1 = (bf16[3,3,128,128]{3,2,1,0:T(8,128)(2,1)S(1)}, bf16[3,3,128,128]{3,2,1,0:T(8,128)(2,1)}, u32[]{:S(2)}) copy-start(bf16[3,3,128,128]{3,2,1,0:T(8,128)(2,1)} %param.18) | copy-start | bytes 884740
  26.5 1.8 %copy-start.2 = (bf16[3,3,128,12]{2,3,1,0:T(8,128)(2,1)S(1)}, bf16[3,3,128,12]{2,3,1,0:T(8,128)(2,1)}, u32[]{:S(2)}) copy-start(bf16[3,3,128,12]{2,3,1,0:T(8,128)(2,1)} %param.19) | copy-start | bytes 82948
  117.8 2.8 %copy-start = (bf16[24576,128]{1,0:T(8,128)(2,1)S(1)}, bf16[24576,128]{1,0:T(8,128)(2,1)}, u32[]{:S(2)}) copy-start(bf16[24576,128]{1,0:T(8,128)(2,1)} %patch_net.1.gathered) | copy-start | bytes 18874372
  120.6 7.5 %copy-start.3 = (s32[16]{0:T(128)S(1)}, s32[16]{0:T(128)}, u32[]{:S(2)}) copy-start(s32[16]{0:T(128)} %param.13) | copy-start | bytes 196
  126.1 10.0 %collective-permute-start = (bf16[12,64,256]{2,1,0:T(8,128)(2,1)S(1)}, bf16[12,64,256]{2,1,0:T(8,128)(2,1)S(1)}, u32[]{:S(2)}, u32[]{:S(2)}) collective-permute-start(bf16[12,64,256]{2,1,0:T(8,128)(2,1)S(1)} %get-tuple-element.8), channel_id=1, source_target_pairs={{0,8},{8,16},{16,24},{24,32},{32,40},{40,48},{48,56},{56,64},{64,7... | collective-permute-start | bytes 1179656 | tf_op jit(solution)/shard_map/ppermute | solution.py:642

commit v3 on v2

v3 whole, which is shorter than its diff:
```python
import math
from functools import partial

import jax
import jax.numpy as jnp
from jax import lax
from jax.experimental import pallas as pl
from jax.experimental.pallas import tpu as pltpu
from jax.sharding import PartitionSpec as P

VARS = 12
CHAN = 128
PS = 128
F = 8
TH = 128
TW = 256
BF = jnp.bfloat16
F32 = jnp.float32
NT, NS = 8, 16
XR = (NT + 2) * NS
KC = 512
GROUP = PS * VARS
UI, UF, UN = 4, 4, 8
MESH = pl.DeviceIdType.MESH


def dot(a, b):
    return jnp.dot(a, b, preferred_element_type=F32)


def dot_nt(a, b):
    return lax.dot_general(a, b, (((1,), (1,)), ((), ())), preferred_element_type=F32)


def split(x):
    hi = x.astype(BF)
    return hi, (x - hi.astype(F32)).astype(BF)


def row_halo(x):
    rows = x.shape[0]
    s = lax.broadcasted_iota(jnp.int32, (rows, NS, CHAN), 1)
    before = jnp.where(s == 0, 0.0, pltpu.roll(x[:, NT - 1], 1, 1))
    after = jnp.where(s == NS - 1, 0.0, pltpu.roll(x[:, 0], NS - 1, 1))
    return before, after


def column_tables(anchor_x, breadth, limit):
    row = lax.broadcasted_iota(jnp.int32, (XR, 256), 0)
    d = lax.broadcasted_iota(jnp.int32, (XR, 256), 1)
    j = (row % NS) * NT + row // NS - 1
    good = (j >= 0) & (j < PS)
    x = (anchor_x + j).astype(F32)
    at = jnp.clip((x + 0.5) * (1.0 / F) - 0.5, 0.0, limit - 1.0)
    hat = jnp.maximum(0.0, 1.0 - jnp.abs(at - d.astype(F32)))
    hat = jnp.where(good, hat, 0.0).astype(BF)
    lane = d[:, :128]
    angle = x[:, :128] * (2.0 * math.pi / breadth)
    pos = jnp.where(lane == 13, jnp.sin(angle), jnp.where(lane == 14, jnp.cos(angle), 0.0))
    pos = jnp.where(lane == 12, 1.0, pos)
    pos = jnp.where(good[:, :128], pos, 0.0)
    return hat, jnp.concatenate([pos, jnp.zeros((XR, KC - 128), F32)], axis=1)


def row_tables(anchor_y, c0, height, limit, loc_ref, pos_ref):
    g = lax.broadcasted_iota(jnp.int32, (16, 256), 0)
    lane = lax.broadcasted_iota(jnp.int32, (16, 256), 1)
    k, ch = (lane % 128) // 16, lane % 16
    i = 8 * g + 4 * (lane // 128) - 1 + k
    good = (i >= 0) & (i < PS) & (k < 6)
    y = (anchor_y + i).astype(F32)
    loc = jnp.clip((y + 0.5) * (1.0 / F) - 0.5, 0.0, limit - 1.0) - c0.astype(F32)
    loc_ref[...] = jnp.where(good, loc - 14.0, -1000.0)
    angle = y * (2.0 * math.pi / height)
    pos = jnp.where(ch == 12, jnp.sin(angle), jnp.where(ch == 13, jnp.cos(angle), 0.0))
    pos_ref[0] = jnp.where(good, pos, 0.0)
    pos_ref[1] = jnp.where(good, 1.0, 0.0)


def interp_stage(hx, xpos, coarse, loc_ref, pos_ref, xh, xl):
    chi, clo = split(coarse)
    t1 = dot_nt(hx, chi) + dot_nt(hx, clo) + xpos
    hi, lo = split(t1)
    lhs = jnp.concatenate([hi, lo], axis=0)
    v_at = lax.broadcasted_iota(jnp.int32, (16, 256), 0)
    ch_at = lax.broadcasted_iota(jnp.int32, (16, 256), 1) % 16
    diag = jnp.where((v_at == ch_at) & (v_at < VARS), 1.0, 0.0).astype(BF)
    pick_y = jnp.where(v_at == 12, 1.0, 0.0)
    pick_x = jnp.where((v_at == 13) & (ch_at == 14) | (v_at == 14) & (ch_at == 15), 1.0, 0.0)
    one = jnp.ones((16, 256), BF)
    none = jnp.zeros((16, 256), BF)

    def step(g, _):
        loc = jnp.broadcast_to(loc_ref[pl.ds(g, 1)], (16, 256)).astype(BF)
        extra = pick_y * pos_ref[0, pl.ds(g, 1)] + pick_x * pos_ref[1, pl.ds(g, 1)]
        blocks = []
        for c in range(28):
            hat = jnp.maximum(none, one - jnp.abs(loc - BF(c - 14))) * diag
            if c == 0:
                hat = hat + extra.astype(BF)
            blocks.append(hat)
        blocks.append(jnp.zeros((64, 256), BF))
        res = dot(lhs, jnp.concatenate(blocks, axis=0))
        x = res[:XR] + res[XR:]
        for h in range(2):
            xa, xb = split(x[:, h * 128 : h * 128 + 128])
            xh[2 * g + h] = xa.reshape(NT + 2, NS, 128)
            xl[2 * g + h] = xb.reshape(NT + 2, NS, 128)
        return 0

    lax.fori_loop(0, 16, step, 0, unroll=UI)


def first_stage(win, b_in, xh, fa, shift, sums):
    bias = b_in[...]
    sums[...] = jnp.zeros_like(sums)

    def rows(at, n):
        lhs = jnp.concatenate(
            [xh[pl.ds(at, n), dx : dx + 8].reshape(n * 128, 128) for dx in range(3)], axis=1
        )
        return dot(lhs, win[...])

    sample = jnp.mean(rows(16, 1)[:, :128] + bias, axis=0, keepdims=True)
    shift[...] = sample

    def step(it, _):
        acc = rows(4 * it, 4)
        base = shift[...]
        one = jnp.zeros((8, CHAN), F32)
        two = jnp.zeros((8, CHAN), F32)
        for r in range(4):
            x = (acc[:, r * 128 : r * 128 + 128] + bias).astype(BF)
            for b in range(4):
                fa[8 * it + 2 * b + r // 2, r % 2] = x[b * 128 : b * 128 + 128]
            d = (x.astype(F32) - base).reshape(64, 8, CHAN)
            one = one + jnp.sum(d, axis=0)
            two = two + jnp.sum(d * d, axis=0)
        sums[0] += one
        sums[1] += two
        return 0

    lax.fori_loop(0, 8, step, 0, unroll=UF)


def group_mean(x):
    lane = lax.broadcasted_iota(jnp.int32, x.shape, 1)
    total = x
    for k in (1, 2):
        low = (lane // k) % 2 == 0
        total = total + jnp.where(low, pltpu.roll(total, CHAN - k, 1), pltpu.roll(total, k, 1))
    return total * 0.25


def scale_shift(sums, shift, gamma, beta):
    n = float(PS * PS)
    one = jnp.broadcast_to(jnp.sum(sums[0], axis=0, keepdims=True), (8, CHAN)) / n
    two = jnp.broadcast_to(jnp.sum(sums[1], axis=0, keepdims=True), (8, CHAN)) / n
    own_var = jnp.maximum(two - one * one, 0.0)
    mean = one + shift[...]
    g_mean = group_mean(mean)
    off = mean - g_mean
    g_var = group_mean(own_var + off * off)
    scale = gamma[...] / jnp.sqrt(g_var + 1e-05)
    return scale[0:1], (beta[...] - g_mean * scale)[0:1]


def norm_stage(scale, offset, fa, nb):
    half_scale = 0.5 * scale
    half_offset = 0.5 * offset

    def step(p, _):
        x = fa[p].astype(F32).reshape(2, NT, NS, CHAN)
        h = x * half_scale + half_offset
        y = h + h * jnp.tanh(h)
        before, after = row_halo(y)
        for r in range(2):
            at, k = (p, 1) if r == 0 else (p + 1, 0)
            nb[at, k, 1 : NT + 1] = y[r].astype(BF)
            nb[at, k, 0] = before[r].astype(BF)
            nb[at, k, NT + 1] = after[r].astype(BF)
        return 0

    lax.fori_loop(0, 64, step, 0, unroll=UN)


def mid_step(it, wmid, nb, fa, sb):
    p0 = 8 * it
    lhs = []
    for k in range(4):
        for dx in range(3):
            lhs.append(nb[pl.ds(p0 + k // 2, 8), k % 2, dx : dx + 8].reshape(1024, CHAN))
    acc = dot(jnp.concatenate(lhs, axis=1), wmid[...])
    for r in range(2):
        x = acc[:, r * 128 : r * 128 + 128] + fa[pl.ds(p0, 8), r].astype(F32).reshape(1024, CHAN)
        x = x.reshape(8, NT, NS, CHAN)
        before, after = row_halo(x)
        for b in range(8):
            at = 2 * b + r + 1
            q, k = 4 * it + at // 4, at % 4
            sb[q, k, 1 : NT + 1] = x[b].astype(BF)
            sb[q, k, 0] = before[b].astype(BF)
            sb[q, k, NT + 1] = after[b].astype(BF)


def out_step(it, wout, sb, xh, xl):
    g0 = 4 * it
    lhs = [sb[pl.ds(g0 + k // 4, 4), k % 4].reshape(4 * XR, CHAN) for k in range(6)]
    lhs.append(xh[pl.ds(g0, 4)].reshape(4 * XR, CHAN))
    lhs.append(xl[pl.ds(g0, 4)].reshape(4 * XR, CHAN))
    acc = dot(jnp.concatenate(lhs, axis=1), wout[...])
    y0 = acc[:, :128].reshape(4, NT + 2, NS, 128)
    y1 = acc[:, 128:].reshape(4, NT + 2, NS, 128)
    centre = pltpu.roll(y0[:, 1 : NT + 1].reshape(512, 128), 64, 1).reshape(4, NT, NS, 128)
    res = y0[:, 0:NT] + centre + y1[:, 2 : NT + 2]
    res = res.reshape(4, 128, 128)
    lane = lax.broadcasted_iota(jnp.int32, (128, 128), 1)
    parts = []
    for h in range(2):
        both = jnp.where(lane < 48, res[2 * h], pltpu.roll(res[2 * h + 1], 48, 1))
        parts.append(jnp.transpose(both)[:96])
    return jnp.concatenate(parts, axis=0).astype(BF)


class CoarseRows:
    def __init__(self, shard, rows, send_sem, recv_sem):
        self.shard, self.rows = shard, rows
        self.send_sem, self.recv_sem = send_sem, recv_sem
        self.r, self.p = lax.axis_index("region"), lax.axis_index("patch")
        self.n_r, self.n_p = lax.axis_size("region"), lax.axis_size("patch")
        self.has_up, self.has_down = self.r > 0, self.r < self.n_r - 1
        self.feeds_down = (self.p == self.n_p - 1) & self.has_down
        self.feeds_up = (self.p < 5) & self.has_up

    def prepare(self, coarse_state):
        r, n_r, rows = self.r, self.n_r, self.rows
        rows[28:32] = jnp.zeros((4, 16, 256), F32)

        @pl.when(r == 0)
        def _():
            rows[0:2] = jnp.zeros((2, 16, 256), F32)

        @pl.when(r == n_r - 1)
        def _():
            rows[18:28] = jnp.zeros((10, 16, 256), F32)

        for c in range(2):
            self.shard[c, 0:VARS] = coarse_state[:, c, :]
            self.shard[c, VARS:16] = jnp.zeros((16 - VARS, 256), F32)
        rows[pl.ds(2 + 2 * self.p, 2)] = self.shard[...]

    def greet(self):
        r, p, n_p = self.r, self.p, self.n_p
        barrier = pltpu.get_barrier_semaphore()

        def hello(to):
            pl.semaphore_signal(barrier, inc=1, device_id=to, device_id_type=MESH)

        for d in range(1, n_p):
            hello((r, (p + d) % n_p))

        @pl.when(self.has_up)
        def _():
            hello((r - 1, n_p - 1))

        @pl.when(self.has_down)
        def _():
            for k in range(5):
                hello((r + 1, k))

        count = n_p - 1 + jnp.where(self.feeds_down, n_p, 0) + jnp.where(self.feeds_up, n_p, 0)
        pl.semaphore_wait(barrier, count)

    def copy(self, row, key, k, to):
        return pltpu.make_async_remote_copy(
            src_ref=self.shard,
            dst_ref=self.rows.at[pl.ds(row, 2)],
            send_sem=self.send_sem.at[k],
            recv_sem=self.recv_sem.at[key],
            device_id=to,
            device_id_type=MESH,
        )

    def each(self, act):
        r, p, n_p = self.r, self.p, self.n_p

        @pl.when(self.feeds_down)
        def _():
            for k in range(n_p):
                act(self.copy(0, 0, 7 + k, (r + 1, k)))

        @pl.when(self.feeds_up)
        def _():
            for k in range(n_p):
                act(self.copy(18 + 2 * p, 9 + p, 15 + k, (r - 1, k)))

        for d in range(1, n_p):
            act(self.copy(2 + 2 * p, 1 + p, d - 1, (r, (p + d) % n_p)))

    def start(self):
        self.each(lambda c: c.start())

    def finish(self):
        r, p, n_p = self.r, self.p, self.n_p
        for d in range(1, n_p):
            q = (p + d) % n_p
            self.copy(2 + 2 * q, 1 + q, 0, (r, q)).wait_recv()

        @pl.when(self.has_up)
        def _():
            self.copy(0, 0, 0, (r - 1, n_p - 1)).wait_recv()

        @pl.when(self.has_down)
        def _():
            for k in range(5):
                self.copy(18 + 2 * k, 9 + k, 0, (r + 1, k)).wait_recv()

        self.each(lambda c: c.wait_send())


CHUNK = 16 * VARS
HALF = CHUNK // 2


class Sharer:
    def __init__(self, out, g, send_sem, recv_sem, tail_sem, own_sem):
        self.out, self.g = out, g
        self.send_sem, self.recv_sem = send_sem, recv_sem
        self.tail_sem, self.own_sem = tail_sem, own_sem
        p = lax.axis_index("patch")
        z, y = p // 2, p % 2
        self.me = p
        self.fore = ((z + 1) % 4) * 2 + y
        self.back = ((z + 3) % 4) * 2 + y
        self.pair = z * 2 + 1 - y
        self.fore_pair = ((z + 1) % 4) * 2 + 1 - y
        self.back_pair = ((z + 3) % 4) * 2 + 1 - y

    def at(self, owner, q, half=None):
        start = (owner * 16 + q) * CHUNK
        if half is None:
            return self.g.at[pl.ds(pl.multiple_of(start, CHUNK), CHUNK)]
        return self.g.at[pl.ds(pl.multiple_of(start + half * HALF, HALF), HALF)]

    def remote(self, src, dst, stream, sem, to):
        return pltpu.make_async_remote_copy(
            src_ref=src,
            dst_ref=dst,
            send_sem=self.send_sem.at[stream],
            recv_sem=sem,
            device_id={"patch": to},
            device_id_type=MESH,
        )

    def arrived(self, owner, q, stream):
        there = self.at(owner, q)
        self.remote(there, there, stream, self.recv_sem.at[stream, q], self.fore).wait_recv()

    def own(self, q):
        src = self.out.at[pl.ds(pl.multiple_of(q * CHUNK, CHUNK), CHUNK)]
        dst = self.at(self.me, q)
        self.remote(src, dst, 2, self.recv_sem.at[2, q], self.pair).start()
        self.remote(src, dst, 0, self.recv_sem.at[0, q], self.fore).start()
        self.remote(src, dst, 1, self.recv_sem.at[1, q], self.back).start()
        pltpu.make_async_copy(src, dst, self.own_sem).start()

    def first(self, q):
        self.arrived(self.pair, q, 2)
        there = self.at(self.pair, q)
        self.remote(there, there, 3, self.recv_sem.at[3, q], self.fore).start()
        self.remote(there, there, 4, self.recv_sem.at[4, q], self.back).start()
        self.arrived(self.back, q, 0)
        there = self.at(self.back, q, 0)
        self.remote(there, there, 5, self.tail_sem.at[0], self.fore).start()
        self.arrived(self.fore, q, 1)
        there = self.at(self.fore, q, 1)
        self.remote(there, there, 6, self.tail_sem.at[1], self.back).start()

    def second(self, q):
        self.arrived(self.back_pair, q, 3)
        there = self.at(self.back_pair, q, 0)
        self.remote(there, there, 7, self.tail_sem.at[2], self.fore).start()
        self.arrived(self.fore_pair, q, 4)
        there = self.at(self.fore_pair, q, 1)
        self.remote(there, there, 8, self.tail_sem.at[3], self.back).start()

    def finish(self):
        whole = self.g.at[pl.ds(0, 2 * GROUP)]
        part = self.g.at[pl.ds(0, GROUP)]
        for k in range(4):
            self.remote(part, part, 5 + k, self.tail_sem.at[k], self.fore).wait()
        for k in range(5):
            self.remote(whole, whole, k, self.tail_sem.at[0], self.fore).wait_send()
        pltpu.make_async_copy(whole, whole, self.own_sem).wait()


def pack_weights(w_in, w_mid, win, wmid):
    zero = jnp.zeros((CHAN, CHAN), BF)
    for dx in range(3):
        for r in range(4):
            cols = slice(r * CHAN, r * CHAN + CHAN)
            parts = [w_in[k - r, dx] if 0 <= k - r < 3 else zero[:16] for k in range(8)]
            win[dx * 128 : dx * 128 + 128, cols] = jnp.concatenate(parts, axis=0)
        for r in range(2):
            cols = slice(r * CHAN, r * CHAN + CHAN)
            for k in range(4):
                at = (k * 3 + dx) * CHAN
                wmid[at : at + CHAN, cols] = w_mid[k - r, dx] if 0 <= k - r < 3 else zero


def patch_kernel(
    grid_size, anchors, coarse_state, w_in, b_in, gamma, beta, w_mid, wout, g,
    shard, rows, loc, pos, win, wmid, out, xh, xl, fa, nb, sb, shift, sums,
    csend_sem, crecv_sem, send_sem, recv_sem, tail_sem, own_sem,
):
    height, breadth, limit_y, limit_x = grid_size
    coarse = CoarseRows(shard, rows, csend_sem, crecv_sem)
    share = Sharer(out, g, send_sem, recv_sem, tail_sem, own_sem)
    coarse.prepare(coarse_state)
    coarse.greet()
    coarse.start()
    pack_weights(w_in, w_mid, win, wmid)
    zero = jnp.zeros((NT + 2, NS, CHAN), BF)
    nb[0, 0] = zero
    nb[64, 1] = zero
    sb[0, 0] = zero
    sb[32, 1] = zero
    c0 = coarse.r * 16 - 2
    coarse.finish()

    def one_slot(slot, _):
        here = share.me * 2 + slot
        row_tables(anchors[here, 0], c0, height, limit_y, loc, pos)
        hx, xpos = column_tables(anchors[here, 1], breadth, limit_x)
        interp_stage(hx, xpos, rows[...].reshape(KC, 256), loc, pos, xh, xl)

        @pl.when(slot == 1)
        def _():
            share.first(6)
            share.first(7)

        first_stage(win, b_in, xh, fa, shift, sums)
        scale, offset = scale_shift(sums, shift, gamma, beta)
        norm_stage(scale, offset, fa, nb)

        def out_chunk(it):
            at = pl.multiple_of((slot * 8 + it) * CHUNK, CHUNK)
            out[pl.ds(at, CHUNK)] = out_step(it, wout, sb, xh, xl)

        mid_step(0, wmid, nb, fa, sb)
        mid_step(1, wmid, nb, fa, sb)

        def step(it, _):
            out_chunk(it - 2)
            mid_step(it, wmid, nb, fa, sb)
            q = slot * 8 + it - 2
            share.own(q)

            @pl.when(it >= 4)
            def _():
                share.first(q - 2)

            @pl.when(slot == 1)
            def _():
                share.second(it - 2)

            return 0

        lax.fori_loop(2, 8, step, 0)
        out_chunk(6)
        out_chunk(7)
        q = slot * 8 + 6
        share.own(q)
        share.own(q + 1)
        share.first(q - 2)
        share.first(q - 1)
        return 0

    lax.fori_loop(0, 2, one_slot, 0)
    share.second(6)
    share.second(7)
    share.first(14)
    share.first(15)

    def drain(q, _):
        share.second(q)
        return 0

    lax.fori_loop(8, 16, drain, 0)
    share.finish()


VM = pl.BlockSpec(memory_space=pltpu.VMEM)
SM = pl.BlockSpec(memory_space=pltpu.SMEM)


def run_patches(grid_size, anchors, coarse_state, weights):
    return pl.pallas_call(
        partial(patch_kernel, grid_size),
        out_shape=jax.ShapeDtypeStruct((16 * GROUP, 128), BF),
        in_specs=[SM] + [VM] * 7,
        out_specs=pl.BlockSpec(memory_space=pltpu.HBM),
        scratch_shapes=[
            pltpu.VMEM((2, 16, 256), F32),
            pltpu.VMEM((32, 16, 256), F32),
            pltpu.VMEM((16, 256), F32),
            pltpu.VMEM((2, 16, 256), F32),
            pltpu.VMEM((3 * 128, 4 * CHAN), BF),
            pltpu.VMEM((12 * CHAN, 2 * CHAN), BF),
            pltpu.VMEM((2 * GROUP, 128), BF),
            pltpu.VMEM((32, NT + 2, NS, 128), BF),
            pltpu.VMEM((32, NT + 2, NS, 128), BF),
            pltpu.VMEM((64, 2, 128, CHAN), BF),
            pltpu.VMEM((65, 2, NT + 2, NS, CHAN), BF),
            pltpu.VMEM((33, 4, NT + 2, NS, CHAN), BF),
            pltpu.VMEM((1, CHAN), F32),
            pltpu.VMEM((2, 8, CHAN), F32),
            pltpu.SemaphoreType.DMA((23,)),
            pltpu.SemaphoreType.DMA((14,)),
            pltpu.SemaphoreType.DMA((9,)),
            pltpu.SemaphoreType.DMA((5, 16)),
            pltpu.SemaphoreType.DMA((4,)),
            pltpu.SemaphoreType.DMA,
        ],
        compiler_params=pltpu.CompilerParams(
            vmem_limit_bytes=56 * 2**20, collective_id=0, has_side_effects=True
        ),
        name="patch_net",
    )(anchors, coarse_state, *weights)


def packed_out(w_out):
    wo = w_out.transpose(0, 2, 1, 3)
    wout = jnp.stack([jnp.pad(wo, ((r, 3 - r), (0, 0), (0, 0), (0, 0))) for r in range(4)], axis=3)
    wout = wout.reshape(6 * CHAN, 3, 48)
    wout = jnp.pad(wout, ((0, 0), (0, 1), (0, 16))).reshape(6 * CHAN, 256)
    row = jnp.arange(128)[:, None]
    col = jnp.arange(256)[None] - 64
    keep = (col >= 0) & (col < 48) & (row % 16 == col % 12) & (row // 16 == col // 12 + 1)
    ident = keep.astype(BF)
    return jnp.concatenate([wout, ident, ident], axis=0)


ACC_ROWS = (3 * TH // 2) * VARS


def place_kernel(anchors, count, blend, gathered, num, cover, over, acc, cov, buf, sem):
    top = lax.axis_index("region") * TH
    left = lax.axis_index("patch") * TW
    acc[...] = jnp.zeros_like(acc)
    cov[...] = jnp.zeros_like(cov)
    lane = lax.broadcasted_iota(jnp.int32, (128, TW), 0)
    x_at = lax.broadcasted_iota(jnp.int32, (128, TW), 1)
    j_at = (lane % NS) * NT + lane // NS
    cov_y = lax.broadcasted_iota(jnp.int32, cov.shape, 0)
    cov_x = lax.broadcasted_iota(jnp.int32, cov.shape, 1)

    def fetch(s, k):
        return pltpu.make_async_copy(gathered.at[pl.ds(s * GROUP, GROUP)], buf.at[k], sem.at[k])

    fetch(0, 0).start()

    def slot(s, _):
        k = s % 2

        @pl.when(s < 15)
        def _():
            fetch(s + 1, 1 - k).start()

        fetch(s, k).wait()
        dy, dx = anchors[s, 0] - top, anchors[s, 1] - left

        @pl.when((s < count[0]) & (dx > -PS) & (dx < TW))
        def _():
            weight = blend[s].astype(F32)
            onehot = jnp.where(x_at - j_at == dx, weight, 0.0).astype(BF)
            par = dy % 2
            base = ((dy - par) // 2) * 24

            def part(n, _):
                y = dot(buf[k, pl.ds(pl.multiple_of(n * 384, 384), 384)], onehot)
                at = pl.multiple_of(base + n * 384, 8)
                for h in range(2):
                    acc[par, h, pl.ds(at, 384)] += y[:, h * 128 : h * 128 + 128]
                return 0

            lax.fori_loop(0, 4, part, 0, unroll=True)
            inside = (cov_y >= dy) & (cov_y < dy + PS) & (cov_x >= dx) & (cov_x < dx + PS)
            cov[...] += jnp.where(inside, weight, 0.0)

        return 0

    lax.fori_loop(0, 16, slot, 0)
    cover[...] = cov[:TH]
    over[VARS] = cov[TH:].astype(BF)
    for v in range(VARS):
        for h in range(2):
            cols = slice(h * 128, h * 128 + 128)
            num[v, :, cols] = acc[0, h, pl.ds(v, TH, VARS)]
            num[v, 1:, cols] += acc[1, h, pl.ds(v, TH - 1, VARS)]
            low = acc[0, h, pl.ds(TH * VARS + v, TH // 2, VARS)]
            low = low + acc[1, h, pl.ds((TH - 1) * VARS + v, TH // 2, VARS)]
            over[v, :, cols] = low.astype(BF)


def run_place(anchors, count, blend, gathered):
    return pl.pallas_call(
        place_kernel,
        out_shape=(
            jax.ShapeDtypeStruct((VARS, TH, TW), F32),
            jax.ShapeDtypeStruct((TH, TW), F32),
            jax.ShapeDtypeStruct((VARS + 1, TH // 2, TW), BF),
        ),
        in_specs=[SM, SM, SM, pl.BlockSpec(memory_space=pltpu.HBM)],
        out_specs=(VM, VM, VM),
        scratch_shapes=[
            pltpu.VMEM((2, 2, ACC_ROWS, 128), F32),
            pltpu.VMEM((3 * TH // 2, TW), F32),
            pltpu.VMEM((2, GROUP, 128), BF),
            pltpu.SemaphoreType.DMA((2,)),
        ],
        compiler_params=pltpu.CompilerParams(vmem_limit_bytes=60 * 2**20),
        name="place",
    )(anchors, count, blend, gathered)


def per_device(coarse_state, anchors, region_count, blend, w_in, b_in, gamma, beta, w_mid, w_out):
    n_region = lax.axis_size("region")
    n_patch = lax.axis_size("patch")
    limit_y = coarse_state.shape[1] * n_region * n_patch
    limit_x = coarse_state.shape[2]
    grid_size = (TH * n_region, TW * n_patch, limit_y, limit_x)
    up = [(i, i + 1) for i in range(n_region - 1)]
    weights = (
        w_in,
        b_in.reshape(1, CHAN),
        gamma.reshape(1, CHAN),
        beta.reshape(1, CHAN),
        w_mid,
        packed_out(w_out),
    )
    gathered = run_patches(grid_size, anchors, coarse_state, weights)
    num, cover, over = run_place(anchors, region_count, blend, gathered)
    low = lax.ppermute(over, "region", up).astype(F32)
    low = jnp.pad(low, ((0, 0), (0, TH // 2), (0, 0)))
    return (num + low[:VARS]) / jnp.maximum(cover + low[VARS], 1.0)


def solution(mesh):
    return jax.shard_map(
        per_device,
        mesh=mesh,
        in_specs=(
            P(None, ("region", "patch"), None),
            P("region", None),
            P("region"),
            P("region"),
            P(),
            P(),
            P(),
            P(),
            P(),
            P(),
        ),
        out_specs=P(None, "region", "patch"),
        check_vma=False,
    )
```

time: 140 us -> 117 us (0.84); the launches traced: 137 us -> 116 us
  local copies, waits for them, and re-layouts: 9.6 us -> 2.88 us
  Pallas kernels: 106 us -> 99.5 us
  other arithmetic: 8.85 us -> 2.63 us
  starting transfers between devices: 3.84 us -> 2.05 us
    pallas_call x2 -> x1, Pallas kernels: 101 us -> 88 us  [run_patches(): pl.pallas_call(partial(patch_kernel, grid_size), out_shape=jax.ShapeDtype...]
    pallas_call x1, Pallas kernels: 5.52 us -> 11.5 us  [run_place(): pl.pallas_call(place_kernel, out_shape=(jax.ShapeDtypeStruct((VARS, TH, T...]
    unnamed x11 -> x5, local copies, waits for them, and re-layouts: 5.38 us -> 1.36 us
    select_n x8 -> x2, other arithmetic: 3.08 us -> 0.02 us  [the longest x1 0.02 us: packed_out(): col % 12]
    ppermute x1 -> x0, starting transfers between devices: 1.92 us -> none  [per_device(): lax.ppermute(jnp.stack([dy - TH, anchors[:, 1], weight]), 'region', up)]
  transfers between devices with their start and end apart: 2 -> 1, of which waited for: 1 -> 1; matrix products, arithmetic and copies ran while one was open for 9% -> 0% of each run, Pallas kernels for 77% -> 0%
where the time goes in v3:
time: 117 us; the launch traced here: 116 us
  Pallas kernels  99.5 us (85%)
  waiting for transfers between devices  8.63 us (7%)
  local copies, waits for them, and re-layouts  2.88 us (2%)
  other arithmetic  2.63 us (2%)
  starting transfers between devices  2.05 us (2%)
    pallas_call x1, Pallas kernels, run_patches(): pl.pallas_call(partial(patch_kernel, grid_size), out_shape=jax.ShapeDtype...  88 us
    pallas_call x1, Pallas kernels, run_place(): pl.pallas_call(place_kernel, out_shape=(jax.ShapeDtypeStruct((VARS, TH, T...  11.5 us
    ppermute x1, waiting for transfers between devices, per_device(): low = lax.ppermute(over, 'region', up).astype(F32)  8.63 us
  transfers between devices with their start and end apart: 1, of which 1 were waited for; matrix products, arithmetic and copies ran while one was open for 0% of the time, Pallas kernels for 0%

profile of v3, /device:TPU:2, one launch (start us, length us, event | category | flops | bytes accessed | tf_op | source)
XLA Modules:
  0.0 116.4 jit_solution(905900343402991263)
XLA Ops:
  0.7 1.4 %copy.16.anchors = s32[16,2]{1,0:T(8,128)} copy(s32[16,2]{0,1:T(2,128)} %param.11) | data formatting | bytes 256 | tf_op args[1]
  2.0 1.0 pad_bitcast_fusion.3
  3.0 0.1 pad_maximum_fusion.1
  3.1 0.1 copy.13
  3.2 0.3 reshape.112
  3.5 0.2 copy.14
  3.7 0.1 and_convert_fusion
  3.8 0.8 pad_maximum_fusion.wout
  4.6 88.0 %patch_net.1.gathered = bf16[24576,128]{1,0:T(8,128)(2,1)} custom-call(s32[16,2]{1,0:T(8,128)} %copy.16.anchors, f32[12,2,256]{2,1,0:T(2,128)} %coarse_state.1, bf16[3,3,16,128]{3,2,1,0:T(8,128)(2,1)} %w_in.1, f32[1,128]{1,0:T(1,128)} %bitcast.23, f32[1,128]{1,0:T(1,128)} %bitcast.24, f32[1,128]{1,0:T(1,128)} %bitcast.25, bf16[3,3,128,128]{3,2,1,0:T(8,128)(2,1)} %w_mid.1, ...), custom_call_target="tpu_custom_call" | custom-call | tf_op jit(solution)/shard_map/patch_net/pallas_call | solution.py:498
  92.6 11.5 %place.1 = (f32[12,128,256]{2,1,0:T(8,128)}, f32[128,256]{1,0:T(8,128)}, bf16[13,64,256]{2,1,0:T(8,128)(2,1)}) custom-call(s32[16,2]{1,0:T(8,128)} %copy.16.anchors, s32[1]{0:T(128)S(6)} %copy.17.count, s32[16]{0:T(128)} %blend.1, bf16[24576,128]{1,0:T(8,128)(2,1)} %patch_net.1.gathered), custom_call_target="tpu_custom_call" | custom-call | tf_op jit(solution)/shard_map/place/pallas_call | solution.py:607
  104.1 0.0 copy-start.1
  104.1 0.0 copy-start
  104.1 2.1 %collective-permute-start = (bf16[13,64,256]{2,1,0:T(8,128)(2,1)}, bf16[13,64,256]{2,1,0:T(8,128)(2,1)S(1)}, u32[]{:S(2)}, u32[]{:S(2)}) collective-permute-start(bf16[13,64,256]{2,1,0:T(8,128)(2,1)} %get-tuple-element.9), channel_id=1, source_target_pairs={{0,8},{8,16},{16,24},{24,32},{32,40},{40,48},{48,56},{56,64},{64,7... | collective-permute-start | bytes 1277960 | tf_op jit(solution)/shard_map/ppermute | solution.py:644
  106.2 8.6 %collective-permute-done = bf16[13,64,256]{2,1,0:T(8,128)(2,1)S(1)} collective-permute-done((bf16[13,64,256]{2,1,0:T(8,128)(2,1)}, bf16[13,64,256]{2,1,0:T(8,128)(2,1)S(1)}, u32[]{:S(2)}, u32[]{:S(2)}) %collective-permute-start) | collective-permute-done | bytes 426016 | tf_op jit(solution)/shard_map/ppermute | solution.py:644
  114.8 0.2 pad_convert_fusion
  114.9 0.0 copy-done.1
  115.0 0.0 copy-done
  115.0 1.4 %fusion = f32[12,128,256]{2,1,0:T(8,128)} fusion(f32[12,128,256]{2,1,0:T(8,128)S(1)} %copy-done, f32[13,128,256]{2,1,0:T(8,128)S(1)} %pad_convert_fusion, f32[128,256]{1,0:T(8,128)S(1)} %fusion.2), kind=kLoop, calls=%fused_computation.1 | loop fusion | flops 786432 | bytes 4849664 | tf_op jit(solution)/shard_map/div | solution.py:646
  (5 shorter events, 0.1 us)
Async XLA Ops:
  104.1 10.9 %copy-start.1 = (f32[128,256]{1,0:T(8,128)S(1)}, f32[128,256]{1,0:T(8,128)}, u32[]{:S(2)}) copy-start(f32[128,256]{1,0:T(8,128)} %get-tuple-element.10) | copy-start | bytes 393220
  104.1 10.9 %copy-start = (f32[12,128,256]{2,1,0:T(8,128)S(1)}, f32[12,128,256]{2,1,0:T(8,128)}, u32[]{:S(2)}) copy-start(f32[12,128,256]{2,1,0:T(8,128)} %get-tuple-element.8) | copy-start | bytes 4718596
  104.1 10.7 %collective-permute-start = (bf16[13,64,256]{2,1,0:T(8,128)(2,1)}, bf16[13,64,256]{2,1,0:T(8,128)(2,1)S(1)}, u32[]{:S(2)}, u32[]{:S(2)}) collective-permute-start(bf16[13,64,256]{2,1,0:T(8,128)(2,1)} %get-tuple-element.9), channel_id=1, source_target_pairs={{0,8},{8,16},{16,24},{24,32},{32,40},{40,48},{48,56},{56,64},{64,7... | collective-permute-start | bytes 1277960 | tf_op jit(solution)/shard_map/ppermute | solution.py:644

commit v4 on v3

--- a/solution.py
+++ b/solution.py
@@ -78,8 +78,7 @@
 
 
 def interp_stage(hx, xpos, coarse, loc_ref, pos_ref, xh, xl):
-    chi, clo = split(coarse)
-    t1 = dot_nt(hx, chi) + dot_nt(hx, clo) + xpos
+    t1 = dot_nt(hx, coarse) + xpos
     hi, lo = split(t1)
     lhs = jnp.concatenate([hi, lo], axis=0)
     v_at = lax.broadcasted_iota(jnp.int32, (16, 256), 0)
@@ -234,19 +233,19 @@
 
     def prepare(self, coarse_state):
         r, n_r, rows = self.r, self.n_r, self.rows
-        rows[28:32] = jnp.zeros((4, 16, 256), F32)
+        rows[28:32] = jnp.zeros((4, 16, 256), BF)
 
         @pl.when(r == 0)
         def _():
-            rows[0:2] = jnp.zeros((2, 16, 256), F32)
+            rows[0:2] = jnp.zeros((2, 16, 256), BF)
 
         @pl.when(r == n_r - 1)
         def _():
-            rows[18:28] = jnp.zeros((10, 16, 256), F32)
-
+            rows[18:28] = jnp.zeros((10, 16, 256), BF)
+
+        pad = jnp.zeros((16 - VARS, 256), F32)
         for c in range(2):
-            self.shard[c, 0:VARS] = coarse_state[:, c, :]
-            self.shard[c, VARS:16] = jnp.zeros((16 - VARS, 256), F32)
+            self.shard[c] = jnp.concatenate([coarse_state[:, c, :], pad], axis=0).astype(BF)
         rows[pl.ds(2 + 2 * self.p, 2)] = self.shard[...]
 
     def greet(self):
@@ -333,8 +332,7 @@
         self.fore = ((z + 1) % 4) * 2 + y
         self.back = ((z + 3) % 4) * 2 + y
         self.pair = z * 2 + 1 - y
-        self.fore_pair = ((z + 1) % 4) * 2 + 1 - y
-        self.back_pair = ((z + 3) % 4) * 2 + 1 - y
+        self.far = ((z + 2) % 4) * 2 + y
 
     def at(self, owner, q, half=None):
         start = (owner * 16 + q) * CHUNK
@@ -367,34 +365,34 @@
     def first(self, q):
         self.arrived(self.pair, q, 2)
         there = self.at(self.pair, q)
-        self.remote(there, there, 3, self.recv_sem.at[3, q], self.fore).start()
-        self.remote(there, there, 4, self.recv_sem.at[4, q], self.back).start()
+        self.remote(there, there, 3, self.tail_sem.at[0], self.fore).start()
+        self.remote(there, there, 4, self.tail_sem.at[1], self.back).start()
         self.arrived(self.back, q, 0)
         there = self.at(self.back, q, 0)
-        self.remote(there, there, 5, self.tail_sem.at[0], self.fore).start()
+        self.remote(there, there, 5, self.recv_sem.at[3, q], self.fore).start()
         self.arrived(self.fore, q, 1)
         there = self.at(self.fore, q, 1)
-        self.remote(there, there, 6, self.tail_sem.at[1], self.back).start()
+        self.remote(there, there, 6, self.recv_sem.at[4, q], self.back).start()
 
     def second(self, q):
-        self.arrived(self.back_pair, q, 3)
-        there = self.at(self.back_pair, q, 0)
-        self.remote(there, there, 7, self.tail_sem.at[2], self.fore).start()
-        self.arrived(self.fore_pair, q, 4)
-        there = self.at(self.fore_pair, q, 1)
-        self.remote(there, there, 8, self.tail_sem.at[3], self.back).start()
+        for half in range(2):
+            there = self.at(self.far, q, half)
+            self.remote(there, there, 5, self.recv_sem.at[3 + half, q], self.fore).wait_recv()
+            self.remote(there, there, 7 + half, self.tail_sem.at[2 + half], self.pair).start()
 
     def finish(self):
         whole = self.g.at[pl.ds(0, 2 * GROUP)]
         part = self.g.at[pl.ds(0, GROUP)]
-        for k in range(4):
-            self.remote(part, part, 5 + k, self.tail_sem.at[k], self.fore).wait()
-        for k in range(5):
+        for k in range(2):
+            self.remote(whole, whole, 3 + k, self.tail_sem.at[k], self.fore).wait()
+            self.remote(part, part, 7 + k, self.tail_sem.at[2 + k], self.fore).wait()
+            self.remote(part, part, 5 + k, self.tail_sem.at[0], self.fore).wait_send()
+        for k in range(3):
             self.remote(whole, whole, k, self.tail_sem.at[0], self.fore).wait_send()
         pltpu.make_async_copy(whole, whole, self.own_sem).wait()
 
 
-def pack_weights(w_in, w_mid, win, wmid):
+def pack_weights(w_in, w_mid, w_out, win, wmid, wout):
     zero = jnp.zeros((CHAN, CHAN), BF)
     for dx in range(3):
         for r in range(4):
@@ -406,11 +404,29 @@
             for k in range(4):
                 at = (k * 3 + dx) * CHAN
                 wmid[at : at + CHAN, cols] = w_mid[k - r, dx] if 0 <= k - r < 3 else zero
+    for k in range(6):
+        halves = []
+        for h in range(2):
+            parts = []
+            for dx in (2 * h, 2 * h + 1):
+                for r in range(4):
+                    used = dx < 3 and 0 <= k - r < 3
+                    parts.append(w_out[k - r, dx].astype(F32) if used else jnp.zeros((VARS, CHAN), F32))
+                parts.append(jnp.zeros((16, CHAN), F32))
+            halves.append(jnp.transpose(jnp.concatenate(parts, axis=0)))
+        wout[k * CHAN : k * CHAN + CHAN] = jnp.concatenate(halves, axis=1).astype(BF)
+    row = lax.broadcasted_iota(jnp.int32, (CHAN, 256), 0)
+    col = lax.broadcasted_iota(jnp.int32, (CHAN, 256), 1) - 64
+    r, v = row // 16 - 1, row % 16
+    keep = (r >= 0) & (r < 4) & (v < VARS) & (col == r * VARS + v)
+    ident = jnp.where(keep, 1.0, 0.0).astype(BF)
+    wout[6 * CHAN : 7 * CHAN] = ident
+    wout[7 * CHAN :] = ident
 
 
 def patch_kernel(
-    grid_size, anchors, coarse_state, w_in, b_in, gamma, beta, w_mid, wout, g,
-    shard, rows, loc, pos, win, wmid, out, xh, xl, fa, nb, sb, shift, sums,
+    grid_size, anchors, coarse_state, w_in, b_in, gamma, beta, w_mid, w_out, g,
+    shard, rows, loc, pos, win, wmid, wout, out, xh, xl, fa, nb, sb, shift, sums,
     csend_sem, crecv_sem, send_sem, recv_sem, tail_sem, own_sem,
 ):
     height, breadth, limit_y, limit_x = grid_size
@@ -419,7 +435,7 @@
     coarse.prepare(coarse_state)
     coarse.greet()
     coarse.start()
-    pack_weights(w_in, w_mid, win, wmid)
+    pack_weights(w_in, w_mid, w_out, win, wmid, wout)
     zero = jnp.zeros((NT + 2, NS, CHAN), BF)
     nb[0, 0] = zero
     nb[64, 1] = zero
@@ -430,8 +446,8 @@
 
     def one_slot(slot, _):
         here = share.me * 2 + slot
-        row_tables(anchors[here, 0], c0, height, limit_y, loc, pos)
-        hx, xpos = column_tables(anchors[here, 1], breadth, limit_x)
+        row_tables(anchors[0, here], c0, height, limit_y, loc, pos)
+        hx, xpos = column_tables(anchors[1, here], breadth, limit_x)
         interp_stage(hx, xpos, rows[...].reshape(KC, 256), loc, pos, xh, xl)
 
         @pl.when(slot == 1)
@@ -501,12 +517,13 @@
         in_specs=[SM] + [VM] * 7,
         out_specs=pl.BlockSpec(memory_space=pltpu.HBM),
         scratch_shapes=[
-            pltpu.VMEM((2, 16, 256), F32),
-            pltpu.VMEM((32, 16, 256), F32),
+            pltpu.VMEM((2, 16, 256), BF),
+            pltpu.VMEM((32, 16, 256), BF),
             pltpu.VMEM((16, 256), F32),
             pltpu.VMEM((2, 16, 256), F32),
             pltpu.VMEM((3 * 128, 4 * CHAN), BF),
             pltpu.VMEM((12 * CHAN, 2 * CHAN), BF),
+            pltpu.VMEM((8 * CHAN, 256), BF),
             pltpu.VMEM((2 * GROUP, 128), BF),
             pltpu.VMEM((32, NT + 2, NS, 128), BF),
             pltpu.VMEM((32, NT + 2, NS, 128), BF),
@@ -529,99 +546,155 @@
     )(anchors, coarse_state, *weights)
 
 
-def packed_out(w_out):
-    wo = w_out.transpose(0, 2, 1, 3)
-    wout = jnp.stack([jnp.pad(wo, ((r, 3 - r), (0, 0), (0, 0), (0, 0))) for r in range(4)], axis=3)
-    wout = wout.reshape(6 * CHAN, 3, 48)
-    wout = jnp.pad(wout, ((0, 0), (0, 1), (0, 16))).reshape(6 * CHAN, 256)
-    row = jnp.arange(128)[:, None]
-    col = jnp.arange(256)[None] - 64
-    keep = (col >= 0) & (col < 48) & (row % 16 == col % 12) & (row // 16 == col // 12 + 1)
-    ident = keep.astype(BF)
-    return jnp.concatenate([wout, ident, ident], axis=0)
-
-
-ACC_ROWS = (3 * TH // 2) * VARS
-
-
-def place_kernel(anchors, count, blend, gathered, num, cover, over, acc, cov, buf, sem):
-    top = lax.axis_index("region") * TH
-    left = lax.axis_index("patch") * TW
-    acc[...] = jnp.zeros_like(acc)
-    cov[...] = jnp.zeros_like(cov)
-    lane = lax.broadcasted_iota(jnp.int32, (128, TW), 0)
-    x_at = lax.broadcasted_iota(jnp.int32, (128, TW), 1)
-    j_at = (lane % NS) * NT + lane // NS
-    cov_y = lax.broadcasted_iota(jnp.int32, cov.shape, 0)
-    cov_x = lax.broadcasted_iota(jnp.int32, cov.shape, 1)
-
-    def fetch(s, k):
-        return pltpu.make_async_copy(gathered.at[pl.ds(s * GROUP, GROUP)], buf.at[k], sem.at[k])
-
-    fetch(0, 0).start()
-
-    def slot(s, _):
-        k = s % 2
-
-        @pl.when(s < 15)
-        def _():
-            fetch(s + 1, 1 - k).start()
-
-        fetch(s, k).wait()
-        dy, dx = anchors[s, 0] - top, anchors[s, 1] - left
-
-        @pl.when((s < count[0]) & (dx > -PS) & (dx < TW))
-        def _():
-            weight = blend[s].astype(F32)
-            onehot = jnp.where(x_at - j_at == dx, weight, 0.0).astype(BF)
-            par = dy % 2
-            base = ((dy - par) // 2) * 24
-
-            def part(n, _):
-                y = dot(buf[k, pl.ds(pl.multiple_of(n * 384, 384), 384)], onehot)
-                at = pl.multiple_of(base + n * 384, 8)
-                for h in range(2):
-                    acc[par, h, pl.ds(at, 384)] += y[:, h * 128 : h * 128 + 128]
-                return 0
-
-            lax.fori_loop(0, 4, part, 0, unroll=True)
-            inside = (cov_y >= dy) & (cov_y < dy + PS) & (cov_x >= dx) & (cov_x < dx + PS)
-            cov[...] += jnp.where(inside, weight, 0.0)
-
-        return 0
-
-    lax.fori_loop(0, 16, slot, 0)
-    cover[...] = cov[:TH]
-    over[VARS] = cov[TH:].astype(BF)
+class Placer:
+    def __init__(self, anchors, count, blend, gathered, first, acc, cov, buf, sem):
+        self.anchors, self.count, self.blend = anchors, count, blend
+        self.gathered, self.first, self.acc, self.cov = gathered, first, acc, cov
+        self.buf, self.sem = buf, sem
+        self.top = lax.axis_index("region") * TH
+        self.left = lax.axis_index("patch") * TW
+        self.size = (PS - first) * VARS
+
+    def where(self, s):
+        return self.anchors[0, s] - self.top, self.anchors[1, s] - self.left
+
+    def meets(self, s):
+        dy, dx = self.where(s)
+        met = (s < self.count[0]) & (dx > -PS) & (dx < TW)
+        return met & (dy > 0) if self.first else met
+
+    def fetch(self, s):
+        at = pl.multiple_of(s * GROUP + self.first * VARS, 96)
+        return pltpu.make_async_copy(
+            self.gathered.at[pl.ds(at, self.size)], self.buf.at[s], self.sem.at[s]
+        )
+
+    def run(self):
+        def start(s, _):
+            @pl.when(self.meets(s))
+            def _():
+                self.fetch(s).start()
+
+            return 0
+
+        lax.fori_loop(0, 16, start, 0)
+        acc, cov = self.acc, self.cov
+        acc[...] = jnp.zeros_like(acc)
+        cov[...] = jnp.zeros_like(cov)
+        lane = lax.broadcasted_iota(jnp.int32, (128, TW), 0)
+        x_at = lax.broadcasted_iota(jnp.int32, (128, TW), 1)
+        shift = x_at - (lane % NS) * NT - lane // NS
+        cov_y = lax.broadcasted_iota(jnp.int32, cov.shape, 0) + self.first
+        cov_x = lax.broadcasted_iota(jnp.int32, cov.shape, 1)
+        step = min(self.size, 768)
+
+        def add(s, _):
+            @pl.when(self.meets(s))
+            def _():
+                dy, dx = self.where(s)
+                weight = self.blend[s].astype(F32)
+                onehot = jnp.where(shift == dx, weight, 0.0).astype(BF)
+                par = dy % 2
+                base = ((dy - par) // 2) * 24
+                inside = (cov_y >= dy) & (cov_y < dy + PS) & (cov_x >= dx) & (cov_x < dx + PS)
+                cov[...] += jnp.where(inside, weight, 0.0)
+                self.fetch(s).wait()
+                for n in range(self.size // step):
+                    y = dot(self.buf[s, n * step : n * step + step], onehot)
+                    at = pl.multiple_of(base + n * step, 8)
+                    for h in range(2):
+                        acc[par, h, pl.ds(at, step)] += y[:, h * 128 : h * 128 + 128]
+
+            return 0
+
+        lax.fori_loop(0, 16, add, 0)
+
+    def rows(self, v, h, start, n):
+        even = self.acc[0, h, pl.ds(start * VARS + v, n, VARS)]
+        odd = self.acc[1, h, pl.ds((start - 1) * VARS + v, n, VARS)]
+        return even + odd
+
+
+def place_own_kernel(anchors, count, blend, gathered, num, cover, acc, cov, buf, sem):
+    placer = Placer(anchors, count, blend, gathered, 0, acc, cov, buf, sem)
+    placer.run()
+    half = TH // 2
+    cover[...] = cov[:half]
+    inverse = 1.0 / jnp.maximum(cov[half:], 1.0)
     for v in range(VARS):
         for h in range(2):
             cols = slice(h * 128, h * 128 + 128)
-            num[v, :, cols] = acc[0, h, pl.ds(v, TH, VARS)]
-            num[v, 1:, cols] += acc[1, h, pl.ds(v, TH - 1, VARS)]
-            low = acc[0, h, pl.ds(TH * VARS + v, TH // 2, VARS)]
-            low = low + acc[1, h, pl.ds((TH - 1) * VARS + v, TH // 2, VARS)]
-            over[v, :, cols] = low.astype(BF)
-
-
-def run_place(anchors, count, blend, gathered):
+            num[v, half:, cols] = placer.rows(v, h, half, half) * inverse[:, cols]
+            num[v, 8:half, cols] = placer.rows(v, h, 8, half - 8)
+            num[v, :8, cols] = acc[0, h, pl.ds(v, 8, VARS)]
+            num[v, 1:8, cols] += acc[1, h, pl.ds(v, 7, VARS)]
+
+
+def finish_kernel(num, cover, low, cover_low, out):
+    inverse = 1.0 / jnp.maximum(cover[...] + cover_low[0].astype(F32), 1.0)
+    out[...] = (num[...] + low[...].astype(F32)) * inverse
+
+
+def run_finish(num, cover, low):
+    half = TH // 2
     return pl.pallas_call(
-        place_kernel,
-        out_shape=(
-            jax.ShapeDtypeStruct((VARS, TH, TW), F32),
-            jax.ShapeDtypeStruct((TH, TW), F32),
-            jax.ShapeDtypeStruct((VARS + 1, TH // 2, TW), BF),
-        ),
+        finish_kernel,
+        grid=(2,),
+        out_shape=jax.ShapeDtypeStruct(num.shape, F32),
+        in_specs=[
+            pl.BlockSpec((VARS // 2, half, TW), lambda i: (i, 0, 0)),
+            pl.BlockSpec((half, TW), lambda i: (0, 0)),
+            pl.BlockSpec((VARS // 2, half, TW), lambda i: (i, 0, 0)),
+            pl.BlockSpec((1, half, TW), lambda i: (VARS, 0, 0)),
+        ],
+        out_specs=pl.BlockSpec((VARS // 2, half, TW), lambda i: (i, 0, 0)),
+        input_output_aliases={0: 0},
+        name="finish",
+    )(num, cover, low, low)
+
+
+def place_over_kernel(anchors, count, blend, gathered, over, acc, cov, buf, sem):
+    half = PS // 2
+    placer = Placer(anchors, count, blend, gathered, half, acc, cov, buf, sem)
+    placer.run()
+    over[VARS] = cov[half:].astype(BF)
+    for v in range(VARS):
+        for h in range(2):
+            over[v, :, h * 128 : h * 128 + 128] = placer.rows(v, h, half, half).astype(BF)
+
+
+def place_call(kernel, first, cov_rows, outs, args, name):
+    lines = (PS - first + TH // 2) * VARS
+    size = (PS - first) * VARS
+    return pl.pallas_call(
+        kernel,
+        out_shape=outs,
         in_specs=[SM, SM, SM, pl.BlockSpec(memory_space=pltpu.HBM)],
-        out_specs=(VM, VM, VM),
+        out_specs=jax.tree.map(lambda _: VM, outs),
         scratch_shapes=[
-            pltpu.VMEM((2, 2, ACC_ROWS, 128), F32),
-            pltpu.VMEM((3 * TH // 2, TW), F32),
-            pltpu.VMEM((2, GROUP, 128), BF),
-            pltpu.SemaphoreType.DMA((2,)),
+            pltpu.VMEM((2, 2, lines, 128), F32),
+            pltpu.VMEM((cov_rows, TW), F32),
+            pltpu.VMEM((16, size, 128), BF),
+            pltpu.SemaphoreType.DMA((16,)),
         ],
         compiler_params=pltpu.CompilerParams(vmem_limit_bytes=60 * 2**20),
-        name="place",
-    )(anchors, count, blend, gathered)
+        cost_estimate=pl.CostEstimate(flops=2 * 8 * size * 128 * 256, bytes_accessed=16 * size * 256, transcendentals=0),
+        name=name,
+    )(*args)
+
+
+def run_place(anchors, count, blend, gathered):
+    args = (anchors, count, blend, gathered)
+    over_shape = jax.ShapeDtypeStruct((VARS + 1, TH // 2, TW), BF)
+    own_shape = (
+        jax.ShapeDtypeStruct((VARS, TH, TW), F32),
+        jax.ShapeDtypeStruct((TH // 2, TW), F32),
+    )
+    over = place_call(place_over_kernel, PS // 2, TH, over_shape, args, "place_over")
+    n = lax.axis_size("region")
+    low = lax.ppermute(over, "region", [(i, i + 1) for i in range(n - 1)])
+    num, cover = place_call(place_own_kernel, 0, TH, own_shape, args, "place_own")
+    return num, cover, low
 
 
 def per_device(coarse_state, anchors, region_count, blend, w_in, b_in, gamma, beta, w_mid, w_out):
@@ -630,20 +703,18 @@
     limit_y = coarse_state.shape[1] * n_region * n_patch
     limit_x = coarse_state.shape[2]
     grid_size = (TH * n_region, TW * n_patch, limit_y, limit_x)
-    up = [(i, i + 1) for i in range(n_region - 1)]
     weights = (
         w_in,
         b_in.reshape(1, CHAN),
         gamma.reshape(1, CHAN),
         beta.reshape(1, CHAN),
         w_mid,
-        packed_out(w_out),
+        w_out.transpose(0, 1, 3, 2),
     )
-    gathered = run_patches(grid_size, anchors, coarse_state, weights)
-    num, cover, over = run_place(anchors, region_count, blend, gathered)
-    low = lax.ppermute(over, "region", up).astype(F32)
-    low = jnp.pad(low, ((0, 0), (0, TH // 2), (0, 0)))
-    return (num + low[:VARS]) / jnp.maximum(cover + low[VARS], 1.0)
+    places = anchors.T
+    gathered = run_patches(grid_size, places, coarse_state, weights)
+    num, cover, low = run_place(places, region_count, blend, gathered)
+    return run_finish(num, cover, low)
 
 
 def solution(mesh):

time: 117 us -> 99.7 us (0.85)
  Pallas kernels: 99.5 us -> 89.9 us
  waiting for transfers between devices: 8.63 us -> 5.51 us
  other arithmetic: 2.63 us -> 0 us
  local copies, waits for them, and re-layouts: 2.88 us -> 0.76 us
    pallas_call x1, Pallas kernels: 88 us -> 82.3 us  [run_patches(): pl.pallas_call(partial(patch_kernel, grid_size), out_shape=jax.ShapeDtype...]
    pallas_call x1 -> x3, Pallas kernels: 11.5 us -> 7.66 us  [the longest x2 5.57 us: place_call(): pl.pallas_call(kernel, out_shape=outs, in_specs=[SM, SM, SM, pl.BlockSpec...]
    ppermute x1, waiting for transfers between devices: 8.63 us -> 5.51 us  [run_place(): low = lax.ppermute(over, 'region', [(i, i + 1) for i in range(n - 1)])]
    div x1 -> x0, other arithmetic: 1.42 us -> none  [per_device(): return (num + low[:VARS]) / jnp.maximum(cover + low[VARS], 1.0)]
  transfers between devices with their start and end apart: 1 -> 1, of which waited for: 1 -> 1; matrix products, arithmetic and copies ran while one was open for 0% -> 0% of each run, Pallas kernels for 0% -> 3%
where the time goes in v4:
time: 99.7 us; the launch traced here: 98.8 us
  Pallas kernels  89.9 us (90%)
  waiting for transfers between devices  5.51 us (6%)
  starting transfers between devices  1.92 us (2%)
    pallas_call x1, Pallas kernels, run_patches(): pl.pallas_call(partial(patch_kernel, grid_size), out_shape=jax.ShapeDtype...  82.3 us
    pallas_call x2, Pallas kernels, place_call(): pl.pallas_call(kernel, out_shape=outs, in_specs=[SM, SM, SM, pl.BlockSpec...  5.57 us
    ppermute x1, waiting for transfers between devices, run_place(): low = lax.ppermute(over, 'region', [(i, i + 1) for i in range(n - 1)])  5.51 us
    pallas_call x1, Pallas kernels, run_finish(): pl.pallas_call(finish_kernel, grid=(2,), out_shape=jax.ShapeDtypeStruct(n...  2.09 us
  transfers between devices with their start and end apart: 1, of which 1 were waited for; matrix products, arithmetic and copies ran while one was open for 0% of the time, Pallas kernels for 3%

profile of v4, /device:TPU:2, one launch (start us, length us, event | category | flops | bytes accessed | tf_op | source)
XLA Modules:
  0.0 98.8 jit_solution(1018818896844189716)
XLA Ops:
  0.7 82.3 %patch_net.1.gathered = bf16[24576,128]{1,0:T(8,128)(2,1)} custom-call(s32[2,16]{1,0:T(2,128)} %bitcast.6, f32[12,2,256]{2,1,0:T(2,128)} %coarse_state.1, bf16[3,3,16,128]{3,2,1,0:T(8,128)(2,1)} %w_in.1, f32[1,128]{1,0:T(1,128)} %bitcast.9, f32[1,128]{1,0:T(1,128)} %bitcast.10, f32[1,128]{1,0:T(1,128)} %bitcast.11, bf16[3,3,128,128]{3,2,1,0:T(8,128)(2,1)} %w_mid.1, ...), custom_call_target="tpu_custom_call" | custom-call | tf_op jit(solution)/shard_map/patch_net/pallas_call | solution.py:514
  82.9 2.5 %place_over.1 = bf16[13,64,256]{2,1,0:T(8,128)(2,1)} custom-call(s32[2,16]{1,0:T(2,128)} %bitcast.7, s32[1]{0:T(128)S(6)} %copy.13.count, s32[16]{0:T(128)} %blend.3, bf16[24576,128]{1,0:T(8,128)(2,1)} %patch_net.1.gathered), custom_call_target="tpu_custom_call" | custom-call | flops 402653184 | bytes 3145728 | tf_op jit(solution)/shard_map/place_over/pallas_call | solution.py:669
  85.4 1.9 %collective-permute-start = (bf16[13,64,256]{2,1,0:T(8,128)(2,1)}, bf16[13,64,256]{2,1,0:T(8,128)(2,1)S(1)}, u32[]{:S(2)}, u32[]{:S(2)}) collective-permute-start(bf16[13,64,256]{2,1,0:T(8,128)(2,1)} %place_over.1), channel_id=1, source_target_pairs={{0,8},{8,16},{16,24},{24,32},{32,40},{40,48},{48,56},{56,64},{64,7... | collective-permute-start | bytes 1277960 | tf_op jit(solution)/shard_map/ppermute | solution.py:695
  87.3 3.1 %place_own.1 = (f32[12,128,256]{2,1,0:T(8,128)}, f32[64,256]{1,0:T(8,128)}) custom-call(s32[2,16]{1,0:T(2,128)} %bitcast.8, s32[1]{0:T(128)S(6)} %copy.13.count, s32[16]{0:T(128)} %blend.3, bf16[24576,128]{1,0:T(8,128)(2,1)} %patch_net.1.gathered), custom_call_target="tpu_custom_call" | custom-call | flops 805306368 | bytes 6291456 | tf_op jit(solution)/shard_map/place_own/pallas_call | solution.py:669
  90.4 5.5 %collective-permute-done.low.cover_low = bf16[13,64,256]{2,1,0:T(8,128)(2,1)S(1)} collective-permute-done((bf16[13,64,256]{2,1,0:T(8,128)(2,1)}, bf16[13,64,256]{2,1,0:T(8,128)(2,1)S(1)}, u32[]{:S(2)}, u32[]{:S(2)}) %collective-permute-start) | collective-permute-done | bytes 426016 | tf_op jit(solution)/shard_map/ppermute | solution.py:695
  95.9 0.0 copy-start
  95.9 0.8 copy-done
  96.7 2.1 %finish.1 = f32[12,128,256]{2,1,0:T(8,128)} custom-call(f32[12,128,256]{2,1,0:T(8,128)} %get-tuple-element.7.num, f32[64,256]{1,0:T(8,128)} %get-tuple-element.8.cover, bf16[13,64,256]{2,1,0:T(8,128)(2,1)} %copy-done, bf16[13,64,256]{2,1,0:T(8,128)(2,1)} %copy-done), custom_call_target="tpu_custom_call", output_to_operand_aliasing={{}: (0, {})} | custom-call | tf_op jit(solution)/shard_map/finish/pallas_call | solution.py:640
Async XLA Ops:
  85.4 10.6 %collective-permute-start = (bf16[13,64,256]{2,1,0:T(8,128)(2,1)}, bf16[13,64,256]{2,1,0:T(8,128)(2,1)S(1)}, u32[]{:S(2)}, u32[]{:S(2)}) collective-permute-start(bf16[13,64,256]{2,1,0:T(8,128)(2,1)} %place_over.1), channel_id=1, source_target_pairs={{0,8},{8,16},{16,24},{24,32},{32,40},{40,48},{48,56},{56,64},{64,7... | collective-permute-start | bytes 1277960 | tf_op jit(solution)/shard_map/ppermute | solution.py:695
  95.9 0.8 copy-start

commit v5 on v4

--- a/solution.py
+++ b/solution.py
@@ -21,6 +21,15 @@
 KC = 512
 GROUP = PS * VARS
 UI, UF, UN = 4, 4, 8
+LAG, LAG2 = 4, 6
+LATER = {
+    "tables": (("pair_on", 0, 4),),
+    "interp": (("far_on", 6, 8), ("pair_on", 4, 8)),
+    "first": (("second", 0, 4),),
+    "norm": (("second", 4, 6),),
+}
+START, COUNT = 2, 2
+DRAIN = (("far_on", 6, 8), ("pair_on", 0, 4), ("second", 0, 4), ("pair_on", 4, 8), ("second", 4, 8))
 MESH = pl.DeviceIdType.MESH
 
 
@@ -77,8 +86,8 @@
     pos_ref[1] = jnp.where(good, 1.0, 0.0)
 
 
-def interp_stage(hx, xpos, coarse, loc_ref, pos_ref, xh, xl):
-    t1 = dot_nt(hx, coarse) + xpos
+def interp_stage(hx, xpos, chi, clo, loc_ref, pos_ref, xh, xl):
+    t1 = dot_nt(hx, chi[...]) + dot_nt(hx, clo[...]) + xpos
     hi, lo = split(t1)
     lhs = jnp.concatenate([hi, lo], axis=0)
     v_at = lax.broadcasted_iota(jnp.int32, (16, 256), 0)
@@ -233,20 +242,25 @@
 
     def prepare(self, coarse_state):
         r, n_r, rows = self.r, self.n_r, self.rows
-        rows[28:32] = jnp.zeros((4, 16, 256), BF)
-
         @pl.when(r == 0)
         def _():
-            rows[0:2] = jnp.zeros((2, 16, 256), BF)
+            rows[0] = jnp.zeros((24, 256), F32)
 
         @pl.when(r == n_r - 1)
         def _():
-            rows[18:28] = jnp.zeros((10, 16, 256), BF)
-
+            rows[9:14] = jnp.zeros((5, 24, 256), F32)
+
+        self.shard[...] = jnp.concatenate([coarse_state[:, c, :] for c in range(2)], axis=0)
+        rows[1 + self.p] = self.shard[...]
+
+    def spread(self, hi, lo):
         pad = jnp.zeros((16 - VARS, 256), F32)
-        for c in range(2):
-            self.shard[c] = jnp.concatenate([coarse_state[:, c, :], pad], axis=0).astype(BF)
-        rows[pl.ds(2 + 2 * self.p, 2)] = self.shard[...]
+        for n in range(14):
+            x = self.rows[n]
+            x = jnp.concatenate([x[:VARS], pad, x[VARS:], pad], axis=0)
+            hi[n * 32 : n * 32 + 32], lo[n * 32 : n * 32 + 32] = split(x)
+        hi[KC - 64 :] = jnp.zeros((64, 256), BF)
+        lo[KC - 64 :] = jnp.zeros((64, 256), BF)
 
     def greet(self):
         r, p, n_p = self.r, self.p, self.n_p
@@ -270,12 +284,12 @@
         count = n_p - 1 + jnp.where(self.feeds_down, n_p, 0) + jnp.where(self.feeds_up, n_p, 0)
         pl.semaphore_wait(barrier, count)
 
-    def copy(self, row, key, k, to):
+    def copy(self, row, k, to):
         return pltpu.make_async_remote_copy(
             src_ref=self.shard,
-            dst_ref=self.rows.at[pl.ds(row, 2)],
+            dst_ref=self.rows.at[row],
             send_sem=self.send_sem.at[k],
-            recv_sem=self.recv_sem.at[key],
+            recv_sem=self.recv_sem.at[row],
             device_id=to,
             device_id_type=MESH,
         )
@@ -286,15 +300,15 @@
         @pl.when(self.feeds_down)
         def _():
             for k in range(n_p):
-                act(self.copy(0, 0, 7 + k, (r + 1, k)))
+                act(self.copy(0, 7 + k, (r + 1, k)))
 
         @pl.when(self.feeds_up)
         def _():
             for k in range(n_p):
-                act(self.copy(18 + 2 * p, 9 + p, 15 + k, (r - 1, k)))
+                act(self.copy(9 + p, 15 + k, (r - 1, k)))
 
         for d in range(1, n_p):
-            act(self.copy(2 + 2 * p, 1 + p, d - 1, (r, (p + d) % n_p)))
+            act(self.copy(1 + p, d - 1, (r, (p + d) % n_p)))
 
     def start(self):
         self.each(lambda c: c.start())
@@ -303,22 +317,21 @@
         r, p, n_p = self.r, self.p, self.n_p
         for d in range(1, n_p):
             q = (p + d) % n_p
-            self.copy(2 + 2 * q, 1 + q, 0, (r, q)).wait_recv()
+            self.copy(1 + q, 0, (r, q)).wait_recv()
 
         @pl.when(self.has_up)
         def _():
-            self.copy(0, 0, 0, (r - 1, n_p - 1)).wait_recv()
+            self.copy(0, 0, (r - 1, n_p - 1)).wait_recv()
 
         @pl.when(self.has_down)
         def _():
             for k in range(5):
-                self.copy(18 + 2 * k, 9 + k, 0, (r + 1, k)).wait_recv()
+                self.copy(9 + k, 0, (r + 1, k)).wait_recv()
 
         self.each(lambda c: c.wait_send())
 
 
 CHUNK = 16 * VARS
-HALF = CHUNK // 2
 
 
 class Sharer:
@@ -334,11 +347,9 @@
         self.pair = z * 2 + 1 - y
         self.far = ((z + 2) % 4) * 2 + y
 
-    def at(self, owner, q, half=None):
-        start = (owner * 16 + q) * CHUNK
-        if half is None:
-            return self.g.at[pl.ds(pl.multiple_of(start, CHUNK), CHUNK)]
-        return self.g.at[pl.ds(pl.multiple_of(start + half * HALF, HALF), HALF)]
+    def at(self, owner, q):
+        start = pl.multiple_of((owner * 16 + q) * CHUNK, CHUNK)
+        return self.g.at[pl.ds(start, CHUNK)]
 
     def remote(self, src, dst, stream, sem, to):
         return pltpu.make_async_remote_copy(
@@ -354,42 +365,71 @@
         there = self.at(owner, q)
         self.remote(there, there, stream, self.recv_sem.at[stream, q], self.fore).wait_recv()
 
-    def own(self, q):
+    def own(self, slot, n):
+        q = slot * 8 + n
         src = self.out.at[pl.ds(pl.multiple_of(q * CHUNK, CHUNK), CHUNK)]
         dst = self.at(self.me, q)
+        even = n % 2 == 0
+        fore, back = jnp.where(even, q, 16), jnp.where(even, 16, q)
         self.remote(src, dst, 2, self.recv_sem.at[2, q], self.pair).start()
-        self.remote(src, dst, 0, self.recv_sem.at[0, q], self.fore).start()
-        self.remote(src, dst, 1, self.recv_sem.at[1, q], self.back).start()
+        self.remote(src, dst, 0, self.recv_sem.at[0, fore], self.fore).start()
+        self.remote(src, dst, 1, self.recv_sem.at[1, back], self.back).start()
+
+    def keep(self, slot):
+        src = self.out.at[pl.ds(pl.multiple_of(slot * GROUP, GROUP), GROUP)]
+        dst = self.g.at[pl.ds(pl.multiple_of((self.me * 2 + slot) * GROUP, GROUP), GROUP)]
         pltpu.make_async_copy(src, dst, self.own_sem).start()
 
-    def first(self, q):
+    def far_on(self, slot, n):
+        q = slot * 8 + n
+        odd = n % 2
+        source = jnp.where(odd == 1, self.fore, self.back)
+        to = jnp.where(odd == 1, self.back, self.fore)
+        self.arrived(source, q, odd)
+        there = self.at(source, q)
+        self.remote(there, there, 5 + odd, self.recv_sem.at[3, q], to).start()
+
+        @pl.when((n == 2) | (n == 5))
+        def _():
+            self.remote(there, there, 9, self.tail_sem.at[3], self.pair).start()
+
+    def pair_on(self, slot, n):
+        q = slot * 8 + n
         self.arrived(self.pair, q, 2)
-        there = self.at(self.pair, q)
-        self.remote(there, there, 3, self.tail_sem.at[0], self.fore).start()
-        self.remote(there, there, 4, self.tail_sem.at[1], self.back).start()
-        self.arrived(self.back, q, 0)
-        there = self.at(self.back, q, 0)
-        self.remote(there, there, 5, self.recv_sem.at[3, q], self.fore).start()
-        self.arrived(self.fore, q, 1)
-        there = self.at(self.fore, q, 1)
-        self.remote(there, there, 6, self.recv_sem.at[4, q], self.back).start()
-
-    def second(self, q):
-        for half in range(2):
-            there = self.at(self.far, q, half)
-            self.remote(there, there, 5, self.recv_sem.at[3 + half, q], self.fore).wait_recv()
-            self.remote(there, there, 7 + half, self.tail_sem.at[2 + half], self.pair).start()
+        mine = self.at(self.pair, q)
+
+        @pl.when(n != 2)
+        def _():
+            self.remote(mine, mine, 3, self.tail_sem.at[0], self.fore).start()
+
+        @pl.when(n != 5)
+        def _():
+            self.remote(mine, mine, 4, self.tail_sem.at[1], self.back).start()
+
+    def second(self, slot, n):
+        q = slot * 8 + n
+        self.arrived(self.far, q, 3)
+        there = self.at(self.far, q)
+        self.remote(there, there, 7, self.tail_sem.at[2], self.pair).start()
 
     def finish(self):
-        whole = self.g.at[pl.ds(0, 2 * GROUP)]
-        part = self.g.at[pl.ds(0, GROUP)]
-        for k in range(2):
-            self.remote(whole, whole, 3 + k, self.tail_sem.at[k], self.fore).wait()
-            self.remote(part, part, 7 + k, self.tail_sem.at[2 + k], self.fore).wait()
-            self.remote(part, part, 5 + k, self.tail_sem.at[0], self.fore).wait_send()
+        def chunks(n):
+            return self.g.at[pl.ds(0, n * CHUNK)]
+
+        def both(stream, sem, n):
+            return self.remote(chunks(n), chunks(n), stream, sem, self.fore)
+
+        both(3, self.tail_sem.at[0], 14).wait()
+        both(4, self.tail_sem.at[1], 14).wait()
+        both(7, self.tail_sem.at[2], 16).wait()
+        both(9, self.tail_sem.at[3], 4).wait()
+        both(0, self.recv_sem.at[0, 16], 8).wait_recv()
+        both(1, self.recv_sem.at[1, 16], 8).wait_recv()
         for k in range(3):
-            self.remote(whole, whole, k, self.tail_sem.at[0], self.fore).wait_send()
-        pltpu.make_async_copy(whole, whole, self.own_sem).wait()
+            both(k, self.tail_sem.at[0], 16).wait_send()
+        both(5, self.tail_sem.at[0], 8).wait_send()
+        both(6, self.tail_sem.at[0], 8).wait_send()
+        pltpu.make_async_copy(chunks(16), chunks(16), self.own_sem).wait()
 
 
 def pack_weights(w_in, w_mid, w_out, win, wmid, wout):
@@ -426,7 +466,7 @@
 
 def patch_kernel(
     grid_size, anchors, coarse_state, w_in, b_in, gamma, beta, w_mid, w_out, g,
-    shard, rows, loc, pos, win, wmid, wout, out, xh, xl, fa, nb, sb, shift, sums,
+    shard, rows, chi, clo, loc, pos, win, wmid, wout, out, xh, xl, fa, nb, sb, shift, sums,
     csend_sem, crecv_sem, send_sem, recv_sem, tail_sem, own_sem,
 ):
     height, breadth, limit_y, limit_x = grid_size
@@ -443,21 +483,36 @@
     sb[32, 1] = zero
     c0 = coarse.r * 16 - 2
     coarse.finish()
+    coarse.spread(chi, clo)
+
+    def hand_on(act, slot, low, high):
+        def one(n, _):
+            getattr(share, act)(slot, n)
+            return 0
+
+        if low < high:
+            lax.fori_loop(low, high, one, 0)
 
     def one_slot(slot, _):
+        def later(name):
+            if name in LATER:
+
+                @pl.when(slot == 1)
+                def _():
+                    for act, low, high in LATER[name]:
+                        hand_on(act, 0, low, high)
+
         here = share.me * 2 + slot
         row_tables(anchors[0, here], c0, height, limit_y, loc, pos)
         hx, xpos = column_tables(anchors[1, here], breadth, limit_x)
-        interp_stage(hx, xpos, rows[...].reshape(KC, 256), loc, pos, xh, xl)
-
-        @pl.when(slot == 1)
-        def _():
-            share.first(6)
-            share.first(7)
-
+        later("tables")
+        interp_stage(hx, xpos, chi, clo, loc, pos, xh, xl)
+        later("interp")
         first_stage(win, b_in, xh, fa, shift, sums)
+        later("first")
         scale, offset = scale_shift(sums, shift, gamma, beta)
         norm_stage(scale, offset, fa, nb)
+        later("norm")
 
         def out_chunk(it):
             at = pl.multiple_of((slot * 8 + it) * CHUNK, CHUNK)
@@ -469,40 +524,34 @@
         def step(it, _):
             out_chunk(it - 2)
             mid_step(it, wmid, nb, fa, sb)
-            q = slot * 8 + it - 2
-            share.own(q)
-
-            @pl.when(it >= 4)
+            share.own(slot, it - 2)
+
+            @pl.when(it >= 2 + LAG)
             def _():
-                share.first(q - 2)
-
-            @pl.when(slot == 1)
+                share.far_on(slot, it - 2 - LAG)
+
+            @pl.when((slot == 1) & (it >= START) & (it < START + COUNT))
             def _():
-                share.second(it - 2)
+                share.second(0, it - START + 8 - COUNT)
+
+            @pl.when((slot == 1) & (it >= 2 + LAG2))
+            def _():
+                share.second(1, it - 2 - LAG2)
 
             return 0
 
         lax.fori_loop(2, 8, step, 0)
         out_chunk(6)
         out_chunk(7)
-        q = slot * 8 + 6
-        share.own(q)
-        share.own(q + 1)
-        share.first(q - 2)
-        share.first(q - 1)
+        share.own(slot, 6)
+        share.own(slot, 7)
+        hand_on("far_on", slot, 6 - LAG, 6)
+        share.keep(slot)
         return 0
 
     lax.fori_loop(0, 2, one_slot, 0)
-    share.second(6)
-    share.second(7)
-    share.first(14)
-    share.first(15)
-
-    def drain(q, _):
-        share.second(q)
-        return 0
-
-    lax.fori_loop(8, 16, drain, 0)
+    for act, low, high in DRAIN:
+        hand_on(act, 1, low, high)
     share.finish()
 
 
@@ -517,8 +566,10 @@
         in_specs=[SM] + [VM] * 7,
         out_specs=pl.BlockSpec(memory_space=pltpu.HBM),
         scratch_shapes=[
-            pltpu.VMEM((2, 16, 256), BF),
-            pltpu.VMEM((32, 16, 256), BF),
+            pltpu.VMEM((24, 256), F32),
+            pltpu.VMEM((14, 24, 256), F32),
+            pltpu.VMEM((KC, 256), BF),
+            pltpu.VMEM((KC, 256), BF),
             pltpu.VMEM((16, 256), F32),
             pltpu.VMEM((2, 16, 256), F32),
             pltpu.VMEM((3 * 128, 4 * CHAN), BF),
@@ -534,8 +585,8 @@
             pltpu.VMEM((2, 8, CHAN), F32),
             pltpu.SemaphoreType.DMA((23,)),
             pltpu.SemaphoreType.DMA((14,)),
-            pltpu.SemaphoreType.DMA((9,)),
-            pltpu.SemaphoreType.DMA((5, 16)),
+            pltpu.SemaphoreType.DMA((10,)),
+            pltpu.SemaphoreType.DMA((4, 17)),
             pltpu.SemaphoreType.DMA((4,)),
             pltpu.SemaphoreType.DMA,
         ],

time: 99.7 us -> 93.1 us (0.934)
  Pallas kernels: 89.9 us -> 85.1 us
  waiting for transfers between devices: 5.51 us -> 4.29 us
    pallas_call x1, Pallas kernels: 82.3 us -> 75.2 us  [run_patches(): pl.pallas_call(partial(patch_kernel, grid_size), out_shape=jax.ShapeDtype...]
    pallas_call x2, Pallas kernels: 5.57 us -> 7.79 us  [place_call(): pl.pallas_call(kernel, out_shape=outs, in_specs=[SM, SM, SM, pl.BlockSpec...]
    ppermute x1, waiting for transfers between devices: 5.51 us -> 4.29 us  [run_place(): low = lax.ppermute(over, 'region', [(i, i + 1) for i in range(n - 1)])]
  transfers between devices with their start and end apart: 1 -> 1, of which waited for: 1 -> 1; matrix products, arithmetic and copies ran while one was open for 0% -> 0% of each run, Pallas kernels for 3% -> 5%
where the time goes in v5:
time: 93.1 us; the launch traced here: 92.8 us
  Pallas kernels  85.1 us (91%)
  waiting for transfers between devices  4.29 us (5%)
  starting transfers between devices  1.92 us (2%)
    pallas_call x1, Pallas kernels, run_patches(): pl.pallas_call(partial(patch_kernel, grid_size), out_shape=jax.ShapeDtype...  75.2 us
    pallas_call x2, Pallas kernels, place_call(): pl.pallas_call(kernel, out_shape=outs, in_specs=[SM, SM, SM, pl.BlockSpec...  7.79 us
    ppermute x1, waiting for transfers between devices, run_place(): low = lax.ppermute(over, 'region', [(i, i + 1) for i in range(n - 1)])  4.29 us
    pallas_call x1, Pallas kernels, run_finish(): pl.pallas_call(finish_kernel, grid=(2,), out_shape=jax.ShapeDtypeStruct(n...  2.09 us
    ppermute x1, starting transfers between devices, run_place(): low = lax.ppermute(over, 'region', [(i, i + 1) for i in range(n - 1)])  1.92 us
  transfers between devices with their start and end apart: 1, of which 1 were waited for; matrix products, arithmetic and copies ran while one was open for 0% of the time, Pallas kernels for 5%

profile of v5, /device:TPU:2, one launch (start us, length us, event | category | flops | bytes accessed | tf_op | source)
XLA Modules:
  0.0 92.8 jit_solution(8073577349266654485)
XLA Ops:
  0.7 75.2 %patch_net.1.gathered = bf16[24576,128]{1,0:T(8,128)(2,1)} custom-call(s32[2,16]{1,0:T(2,128)} %bitcast.6, f32[12,2,256]{2,1,0:T(2,128)} %coarse_state.1, bf16[3,3,16,128]{3,2,1,0:T(8,128)(2,1)} %w_in.1, f32[1,128]{1,0:T(1,128)} %bitcast.9, f32[1,128]{1,0:T(1,128)} %bitcast.10, f32[1,128]{1,0:T(1,128)} %bitcast.11, bf16[3,3,128,128]{3,2,1,0:T(8,128)(2,1)} %w_mid.1, ...), custom_call_target="tpu_custom_call" | custom-call | tf_op jit(solution)/shard_map/patch_net/pallas_call | solution.py:563
  75.9 3.5 %place_over.1 = bf16[13,64,256]{2,1,0:T(8,128)(2,1)} custom-call(s32[2,16]{1,0:T(2,128)} %bitcast.7, s32[1]{0:T(128)S(6)} %copy.13.count, s32[16]{0:T(128)} %blend.3, bf16[24576,128]{1,0:T(8,128)(2,1)} %patch_net.1.gathered), custom_call_target="tpu_custom_call" | custom-call | flops 402653184 | bytes 3145728 | tf_op jit(solution)/shard_map/place_over/pallas_call | solution.py:720
  79.4 1.9 %collective-permute-start = (bf16[13,64,256]{2,1,0:T(8,128)(2,1)}, bf16[13,64,256]{2,1,0:T(8,128)(2,1)S(1)}, u32[]{:S(2)}, u32[]{:S(2)}) collective-permute-start(bf16[13,64,256]{2,1,0:T(8,128)(2,1)} %place_over.1), channel_id=1, source_target_pairs={{0,8},{8,16},{16,24},{24,32},{32,40},{40,48},{48,56},{56,64},{64,7... | collective-permute-start | bytes 1277960 | tf_op jit(solution)/shard_map/ppermute | solution.py:746
  81.3 4.3 %place_own.1 = (f32[12,128,256]{2,1,0:T(8,128)}, f32[64,256]{1,0:T(8,128)}) custom-call(s32[2,16]{1,0:T(2,128)} %bitcast.8, s32[1]{0:T(128)S(6)} %copy.13.count, s32[16]{0:T(128)} %blend.3, bf16[24576,128]{1,0:T(8,128)(2,1)} %patch_net.1.gathered), custom_call_target="tpu_custom_call" | custom-call | flops 805306368 | bytes 6291456 | tf_op jit(solution)/shard_map/place_own/pallas_call | solution.py:720
  85.6 4.3 %collective-permute-done.low.cover_low = bf16[13,64,256]{2,1,0:T(8,128)(2,1)S(1)} collective-permute-done((bf16[13,64,256]{2,1,0:T(8,128)(2,1)}, bf16[13,64,256]{2,1,0:T(8,128)(2,1)S(1)}, u32[]{:S(2)}, u32[]{:S(2)}) %collective-permute-start) | collective-permute-done | bytes 426016 | tf_op jit(solution)/shard_map/ppermute | solution.py:746
  89.9 0.0 copy-start
  89.9 0.8 copy-done
  90.7 2.1 %finish.1 = f32[12,128,256]{2,1,0:T(8,128)} custom-call(f32[12,128,256]{2,1,0:T(8,128)} %get-tuple-element.7.num, f32[64,256]{1,0:T(8,128)} %get-tuple-element.8.cover, bf16[13,64,256]{2,1,0:T(8,128)(2,1)} %copy-done, bf16[13,64,256]{2,1,0:T(8,128)(2,1)} %copy-done), custom_call_target="tpu_custom_call", output_to_operand_aliasing={{}: (0, {})} | custom-call | tf_op jit(solution)/shard_map/finish/pallas_call | solution.py:691
Async XLA Ops:
  79.4 10.6 %collective-permute-start = (bf16[13,64,256]{2,1,0:T(8,128)(2,1)}, bf16[13,64,256]{2,1,0:T(8,128)(2,1)S(1)}, u32[]{:S(2)}, u32[]{:S(2)}) collective-permute-start(bf16[13,64,256]{2,1,0:T(8,128)(2,1)} %place_over.1), channel_id=1, source_target_pairs={{0,8},{8,16},{16,24},{24,32},{32,40},{40,48},{48,56},{56,64},{64,7... | collective-permute-start | bytes 1277960 | tf_op jit(solution)/shard_map/ppermute | solution.py:746
  89.9 0.8 copy-start

commit v6 on v5

--- a/solution.py
+++ b/solution.py
@@ -20,7 +20,8 @@
 XR = (NT + 2) * NS
 KC = 512
 GROUP = PS * VARS
-UI, UF, UN = 4, 4, 8
+UI, UF, UN = 8, 8, 16
+FINISH = 2
 LAG, LAG2 = 4, 6
 LATER = {
     "tables": (("pair_on", 0, 4),),
@@ -68,7 +69,7 @@
     pos = jnp.where(lane == 13, jnp.sin(angle), jnp.where(lane == 14, jnp.cos(angle), 0.0))
     pos = jnp.where(lane == 12, 1.0, pos)
     pos = jnp.where(good[:, :128], pos, 0.0)
-    return hat, jnp.concatenate([pos, jnp.zeros((XR, KC - 128), F32)], axis=1)
+    return hat, pos
 
 
 def row_tables(anchor_y, c0, height, limit, loc_ref, pos_ref):
@@ -87,7 +88,8 @@
 
 
 def interp_stage(hx, xpos, chi, clo, loc_ref, pos_ref, xh, xl):
-    t1 = dot_nt(hx, chi[...]) + dot_nt(hx, clo[...]) + xpos
+    t1 = dot_nt(hx, chi[...]) + dot_nt(hx, clo[...])
+    t1 = jnp.concatenate([t1[:, :128] + xpos, t1[:, 128:]], axis=1)
     hi, lo = split(t1)
     lhs = jnp.concatenate([hi, lo], axis=0)
     v_at = lax.broadcasted_iota(jnp.int32, (16, 256), 0)
@@ -466,7 +468,7 @@
 
 def patch_kernel(
     grid_size, anchors, coarse_state, w_in, b_in, gamma, beta, w_mid, w_out, g,
-    shard, rows, chi, clo, loc, pos, win, wmid, wout, out, xh, xl, fa, nb, sb, shift, sums,
+    shard, rows, chi, clo, hx, xpos, loc, pos, win, wmid, wout, out, xh, xl, fa, nb, sb, shift, sums,
     csend_sem, crecv_sem, send_sem, recv_sem, tail_sem, own_sem,
 ):
     height, breadth, limit_y, limit_x = grid_size
@@ -482,6 +484,14 @@
     sb[0, 0] = zero
     sb[32, 1] = zero
     c0 = coarse.r * 16 - 2
+
+    def tables(slot, _):
+        here = share.me * 2 + slot
+        row_tables(anchors[0, here], c0, height, limit_y, loc.at[slot], pos.at[slot])
+        hx[slot], xpos[slot] = column_tables(anchors[1, here], breadth, limit_x)
+        return 0
+
+    lax.fori_loop(0, 2, tables, 0)
     coarse.finish()
     coarse.spread(chi, clo)
 
@@ -502,11 +512,8 @@
                     for act, low, high in LATER[name]:
                         hand_on(act, 0, low, high)
 
-        here = share.me * 2 + slot
-        row_tables(anchors[0, here], c0, height, limit_y, loc, pos)
-        hx, xpos = column_tables(anchors[1, here], breadth, limit_x)
         later("tables")
-        interp_stage(hx, xpos, chi, clo, loc, pos, xh, xl)
+        interp_stage(hx[slot], xpos[slot], chi, clo, loc.at[slot], pos.at[slot], xh, xl)
         later("interp")
         first_stage(win, b_in, xh, fa, shift, sums)
         later("first")
@@ -570,8 +577,10 @@
             pltpu.VMEM((14, 24, 256), F32),
             pltpu.VMEM((KC, 256), BF),
             pltpu.VMEM((KC, 256), BF),
-            pltpu.VMEM((16, 256), F32),
+            pltpu.VMEM((2, XR, 256), BF),
+            pltpu.VMEM((2, XR, 128), F32),
             pltpu.VMEM((2, 16, 256), F32),
+            pltpu.VMEM((2, 2, 16, 256), F32),
             pltpu.VMEM((3 * 128, 4 * CHAN), BF),
             pltpu.VMEM((12 * CHAN, 2 * CHAN), BF),
             pltpu.VMEM((8 * CHAN, 256), BF),
@@ -666,11 +675,10 @@
         return even + odd
 
 
-def place_own_kernel(anchors, count, blend, gathered, num, cover, acc, cov, buf, sem):
+def place_own_kernel(anchors, count, blend, gathered, num, acc, cov, buf, sem):
     placer = Placer(anchors, count, blend, gathered, 0, acc, cov, buf, sem)
     placer.run()
     half = TH // 2
-    cover[...] = cov[:half]
     inverse = 1.0 / jnp.maximum(cov[half:], 1.0)
     for v in range(VARS):
         for h in range(2):
@@ -681,27 +689,40 @@
             num[v, 1:8, cols] += acc[1, h, pl.ds(v, 7, VARS)]
 
 
-def finish_kernel(num, cover, low, cover_low, out):
-    inverse = 1.0 / jnp.maximum(cover[...] + cover_low[0].astype(F32), 1.0)
-    out[...] = (num[...] + low[...].astype(F32)) * inverse
-
-
-def run_finish(num, cover, low):
-    half = TH // 2
+def finish_kernel(anchors, count, blend, num, low, cover_low, out, inverse):
+    @pl.when(pl.program_id(0) == 0)
+    def _():
+        top = lax.axis_index("region") * TH
+        left = lax.axis_index("patch") * TW
+        y = lax.broadcasted_iota(jnp.int32, inverse.shape, 0) + top
+        x = lax.broadcasted_iota(jnp.int32, inverse.shape, 1) + left
+        inverse[...] = cover_low[0].astype(F32)
+
+        def add(s, _):
+            dy, dx = y - anchors[0, s], x - anchors[1, s]
+            weight = jnp.where(s < count[0], blend[s], 0).astype(F32)
+            inverse[...] += jnp.where((dy >= 0) & (dy < PS) & (dx >= 0) & (dx < PS), weight, 0.0)
+            return 0
+
+        lax.fori_loop(0, 16, add, 0)
+        inverse[...] = 1.0 / jnp.maximum(inverse[...], 1.0)
+
+    out[...] = (num[...] + low[...].astype(F32)) * inverse[...]
+
+
+def run_finish(places, count, blend, num, low):
+    half, n = TH // 2, VARS // FINISH
+    own = pl.BlockSpec((n, half, TW), lambda i: (i, 0, 0))
     return pl.pallas_call(
         finish_kernel,
-        grid=(2,),
+        grid=(FINISH,),
         out_shape=jax.ShapeDtypeStruct(num.shape, F32),
-        in_specs=[
-            pl.BlockSpec((VARS // 2, half, TW), lambda i: (i, 0, 0)),
-            pl.BlockSpec((half, TW), lambda i: (0, 0)),
-            pl.BlockSpec((VARS // 2, half, TW), lambda i: (i, 0, 0)),
-            pl.BlockSpec((1, half, TW), lambda i: (VARS, 0, 0)),
-        ],
-        out_specs=pl.BlockSpec((VARS // 2, half, TW), lambda i: (i, 0, 0)),
-        input_output_aliases={0: 0},
+        in_specs=[SM, SM, SM, own, own, pl.BlockSpec((1, half, TW), lambda i: (VARS, 0, 0))],
+        out_specs=own,
+        scratch_shapes=[pltpu.VMEM((half, TW), F32)],
+        input_output_aliases={3: 0},
         name="finish",
-    )(num, cover, low, low)
+    )(places, count, blend, num, low, low)
 
 
 def place_over_kernel(anchors, count, blend, gathered, over, acc, cov, buf, sem):
@@ -737,15 +758,12 @@
 def run_place(anchors, count, blend, gathered):
     args = (anchors, count, blend, gathered)
     over_shape = jax.ShapeDtypeStruct((VARS + 1, TH // 2, TW), BF)
-    own_shape = (
-        jax.ShapeDtypeStruct((VARS, TH, TW), F32),
-        jax.ShapeDtypeStruct((TH // 2, TW), F32),
-    )
+    own_shape = jax.ShapeDtypeStruct((VARS, TH, TW), F32)
     over = place_call(place_over_kernel, PS // 2, TH, over_shape, args, "place_over")
     n = lax.axis_size("region")
     low = lax.ppermute(over, "region", [(i, i + 1) for i in range(n - 1)])
-    num, cover = place_call(place_own_kernel, 0, TH, own_shape, args, "place_own")
-    return num, cover, low
+    num = place_call(place_own_kernel, 0, TH, own_shape, args, "place_own")
+    return num, low
 
 
 def per_device(coarse_state, anchors, region_count, blend, w_in, b_in, gamma, beta, w_mid, w_out):
@@ -764,8 +782,8 @@
     )
     places = anchors.T
     gathered = run_patches(grid_size, places, coarse_state, weights)
-    num, cover, low = run_place(places, region_count, blend, gathered)
-    return run_finish(num, cover, low)
+    num, low = run_place(places, region_count, blend, gathered)
+    return run_finish(places, region_count, blend, num, low)
 
 
 def solution(mesh):

time: 93.1 us -> 91.2 us (0.980)
  Pallas kernels: 85.1 us -> 83.8 us
    pallas_call x1, Pallas kernels: 75.2 us -> 73.1 us  [run_patches(): pl.pallas_call(partial(patch_kernel, grid_size), out_shape=jax.ShapeDtype...]
where the time goes in v6:
time: 91.2 us; the launch traced here: 91.1 us
  Pallas kernels  83.8 us (92%)
  waiting for transfers between devices  3.96 us (4%)
  starting transfers between devices  1.92 us (2%)
    pallas_call x1, Pallas kernels, run_patches(): pl.pallas_call(partial(patch_kernel, grid_size), out_shape=jax.ShapeDtype...  73.1 us
    pallas_call x2, Pallas kernels, place_call(): pl.pallas_call(kernel, out_shape=outs, in_specs=[SM, SM, SM, pl.BlockSpec...  8.35 us
    ppermute x1, waiting for transfers between devices, run_place(): low = lax.ppermute(over, 'region', [(i, i + 1) for i in range(n - 1)])  3.96 us
    pallas_call x1, Pallas kernels, run_finish(): pl.pallas_call(finish_kernel, grid=(FINISH,), out_shape=jax.ShapeDtypeStr...  2.31 us
    ppermute x1, starting transfers between devices, run_place(): low = lax.ppermute(over, 'region', [(i, i + 1) for i in range(n - 1)])  1.92 us
  transfers between devices with their start and end apart: 1, of which 1 were waited for; matrix products, arithmetic and copies ran while one was open for 0% of the time, Pallas kernels for 5%

profile of v6, /device:TPU:2, one launch (start us, length us, event | category | flops | bytes accessed | tf_op | source)
XLA Modules:
  0.0 91.1 jit_solution(11404491412609624203)
XLA Ops:
  0.7 73.1 %patch_net.1.gathered = bf16[24576,128]{1,0:T(8,128)(2,1)} custom-call(s32[2,16]{1,0:T(2,128)} %bitcast.6, f32[12,2,256]{2,1,0:T(2,128)} %coarse_state.1, bf16[3,3,16,128]{3,2,1,0:T(8,128)(2,1)} %w_in.1, f32[1,128]{1,0:T(1,128)} %bitcast.10, f32[1,128]{1,0:T(1,128)} %bitcast.11, f32[1,128]{1,0:T(1,128)} %bitcast.12, bf16[3,3,128,128]{3,2,1,0:T(8,128)(2,1)} %w_mid.1, ...), custom_call_target="tpu_custom_call" | custom-call | tf_op jit(solution)/shard_map/patch_net/pallas_call | solution.py:570
  73.8 3.7 %place_over.1 = bf16[13,64,256]{2,1,0:T(8,128)(2,1)} custom-call(s32[2,16]{1,0:T(2,128)} %bitcast.7, s32[1]{0:T(128)S(6)} %copy.13.count, s32[16]{0:T(128)} %blend.5, bf16[24576,128]{1,0:T(8,128)(2,1)} %patch_net.1.gathered), custom_call_target="tpu_custom_call" | custom-call | flops 402653184 | bytes 3145728 | tf_op jit(solution)/shard_map/place_over/pallas_call | solution.py:741
  77.5 1.9 %collective-permute-start = (bf16[13,64,256]{2,1,0:T(8,128)(2,1)}, bf16[13,64,256]{2,1,0:T(8,128)(2,1)S(1)}, u32[]{:S(2)}, u32[]{:S(2)}) collective-permute-start(bf16[13,64,256]{2,1,0:T(8,128)(2,1)} %place_over.1), channel_id=1, source_target_pairs={{0,8},{8,16},{16,24},{24,32},{32,40},{40,48},{48,56},{56,64},{64,7... | collective-permute-start | bytes 1277960 | tf_op jit(solution)/shard_map/ppermute | solution.py:764
  79.4 4.7 %place_own.1.num = f32[12,128,256]{2,1,0:T(8,128)} custom-call(s32[2,16]{1,0:T(2,128)} %bitcast.8, s32[1]{0:T(128)S(6)} %copy.13.count, s32[16]{0:T(128)} %blend.5, bf16[24576,128]{1,0:T(8,128)(2,1)} %patch_net.1.gathered), custom_call_target="tpu_custom_call" | custom-call | flops 805306368 | bytes 6291456 | tf_op jit(solution)/shard_map/place_own/pallas_call | solution.py:741
  84.1 4.0 %collective-permute-done.low.cover_low = bf16[13,64,256]{2,1,0:T(8,128)(2,1)S(1)} collective-permute-done((bf16[13,64,256]{2,1,0:T(8,128)(2,1)}, bf16[13,64,256]{2,1,0:T(8,128)(2,1)S(1)}, u32[]{:S(2)}, u32[]{:S(2)}) %collective-permute-start) | collective-permute-done | bytes 426016 | tf_op jit(solution)/shard_map/ppermute | solution.py:764
  88.0 0.0 copy-start
  88.0 0.8 copy-done
  88.8 2.3 %finish.1 = f32[12,128,256]{2,1,0:T(8,128)} custom-call(s32[2,16]{1,0:T(2,128)} %bitcast.9, s32[1]{0:T(128)S(6)} %copy.13.count, s32[16]{0:T(128)} %blend.5, f32[12,128,256]{2,1,0:T(8,128)} %place_own.1.num, bf16[13,64,256]{2,1,0:T(8,128)(2,1)} %copy-done, bf16[13,64,256]{2,1,0:T(8,128)(2,1)} %copy-done), custom_call_target="tpu_custom_call", output_to_operand_aliasing={{}: (3, {})} | custom-call | tf_op jit(solution)/shard_map/finish/pallas_call | solution.py:716
Async XLA Ops:
  77.5 10.6 %collective-permute-start = (bf16[13,64,256]{2,1,0:T(8,128)(2,1)}, bf16[13,64,256]{2,1,0:T(8,128)(2,1)S(1)}, u32[]{:S(2)}, u32[]{:S(2)}) collective-permute-start(bf16[13,64,256]{2,1,0:T(8,128)(2,1)} %place_over.1), channel_id=1, source_target_pairs={{0,8},{8,16},{16,24},{24,32},{32,40},{40,48},{48,56},{56,64},{64,7... | collective-permute-start | bytes 1277960 | tf_op jit(solution)/shard_map/ppermute | solution.py:764
  88.0 0.8 copy-start

commit v7 on v6

--- a/solution.py
+++ b/solution.py
@@ -30,7 +30,7 @@
     "norm": (("second", 4, 6),),
 }
 START, COUNT = 2, 2
-DRAIN = (("far_on", 6, 8), ("pair_on", 0, 4), ("second", 0, 4), ("pair_on", 4, 8), ("second", 4, 8))
+DRAIN = (("far_on", 6, 8), ("second", 0, 2), ("pair_on", 0, 4), ("second", 2, 4), ("pair_on", 4, 8), ("second", 4, 8))
 MESH = pl.DeviceIdType.MESH
 
 
@@ -330,6 +330,7 @@
             for k in range(5):
                 self.copy(9 + k, 0, (r + 1, k)).wait_recv()
 
+    def sent(self):
         self.each(lambda c: c.wait_send())
 
 
@@ -553,13 +554,15 @@
         share.own(slot, 6)
         share.own(slot, 7)
         hand_on("far_on", slot, 6 - LAG, 6)
-        share.keep(slot)
         return 0
 
     lax.fori_loop(0, 2, one_slot, 0)
+    share.keep(0)
+    share.keep(1)
     for act, low, high in DRAIN:
         hand_on(act, 1, low, high)
     share.finish()
+    coarse.sent()
 
 
 VM = pl.BlockSpec(memory_space=pltpu.VMEM)
@@ -644,9 +647,9 @@
         lane = lax.broadcasted_iota(jnp.int32, (128, TW), 0)
         x_at = lax.broadcasted_iota(jnp.int32, (128, TW), 1)
         shift = x_at - (lane % NS) * NT - lane // NS
-        cov_y = lax.broadcasted_iota(jnp.int32, cov.shape, 0) + self.first
+        cov_y = lax.broadcasted_iota(jnp.int32, cov.shape, 0) + (TH if self.first else TH // 2)
         cov_x = lax.broadcasted_iota(jnp.int32, cov.shape, 1)
-        step = min(self.size, 768)
+        step = self.size // 2
 
         def add(s, _):
             @pl.when(self.meets(s))
@@ -659,12 +662,19 @@
                 inside = (cov_y >= dy) & (cov_y < dy + PS) & (cov_x >= dx) & (cov_x < dx + PS)
                 cov[...] += jnp.where(inside, weight, 0.0)
                 self.fetch(s).wait()
-                for n in range(self.size // step):
+
+                def part(n):
                     y = dot(self.buf[s, n * step : n * step + step], onehot)
                     at = pl.multiple_of(base + n * step, 8)
                     for h in range(2):
                         acc[par, h, pl.ds(at, step)] += y[:, h * 128 : h * 128 + 128]
 
+                if self.first:
+                    pl.when(dy > PS // 4)(lambda: part(0))
+                else:
+                    part(0)
+                part(1)
+
             return 0
 
         lax.fori_loop(0, 16, add, 0)
@@ -679,7 +689,7 @@
     placer = Placer(anchors, count, blend, gathered, 0, acc, cov, buf, sem)
     placer.run()
     half = TH // 2
-    inverse = 1.0 / jnp.maximum(cov[half:], 1.0)
+    inverse = 1.0 / jnp.maximum(cov[...], 1.0)
     for v in range(VARS):
         for h in range(2):
             cols = slice(h * 128, h * 128 + 128)
@@ -729,7 +739,7 @@
     half = PS // 2
     placer = Placer(anchors, count, blend, gathered, half, acc, cov, buf, sem)
     placer.run()
-    over[VARS] = cov[half:].astype(BF)
+    over[VARS] = cov[...].astype(BF)
     for v in range(VARS):
         for h in range(2):
             over[v, :, h * 128 : h * 128 + 128] = placer.rows(v, h, half, half).astype(BF)
@@ -759,10 +769,10 @@
     args = (anchors, count, blend, gathered)
     over_shape = jax.ShapeDtypeStruct((VARS + 1, TH // 2, TW), BF)
     own_shape = jax.ShapeDtypeStruct((VARS, TH, TW), F32)
-    over = place_call(place_over_kernel, PS // 2, TH, over_shape, args, "place_over")
+    over = place_call(place_over_kernel, PS // 2, TH // 2, over_shape, args, "place_over")
     n = lax.axis_size("region")
     low = lax.ppermute(over, "region", [(i, i + 1) for i in range(n - 1)])
-    num = place_call(place_own_kernel, 0, TH, own_shape, args, "place_own")
+    num = place_call(place_own_kernel, 0, TH // 2, own_shape, args, "place_own")
     return num, low
 
 

time: 91.2 us -> 91.7 us (level); the launches traced: 91.1 us -> 90.7 us
  Pallas kernels: 83.8 us -> 82.6 us
    pallas_call x2, Pallas kernels: 8.35 us -> 7.16 us  [place_call(): pl.pallas_call(kernel, out_shape=outs, in_specs=[SM, SM, SM, pl.BlockSpec...]
  transfers between devices with their start and end apart: 1 -> 1, of which waited for: 1 -> 1; matrix products, arithmetic and copies ran while one was open for 0% -> 0% of each run, Pallas kernels for 5% -> 4%
where the time goes in v7:
time: 91.7 us; the launch traced here: 90.7 us
  Pallas kernels  82.6 us (90%)
  waiting for transfers between devices  4.74 us (5%)
  starting transfers between devices  1.92 us (2%)
    pallas_call x1, Pallas kernels, run_patches(): pl.pallas_call(partial(patch_kernel, grid_size), out_shape=jax.ShapeDtype...  73.1 us
    pallas_call x2, Pallas kernels, place_call(): pl.pallas_call(kernel, out_shape=outs, in_specs=[SM, SM, SM, pl.BlockSpec...  7.16 us
    ppermute x1, waiting for transfers between devices, run_place(): low = lax.ppermute(over, 'region', [(i, i + 1) for i in range(n - 1)])  4.74 us
    pallas_call x1, Pallas kernels, run_finish(): pl.pallas_call(finish_kernel, grid=(FINISH,), out_shape=jax.ShapeDtypeStr...  2.31 us
    ppermute x1, starting transfers between devices, run_place(): low = lax.ppermute(over, 'region', [(i, i + 1) for i in range(n - 1)])  1.92 us
  transfers between devices with their start and end apart: 1, of which 1 were waited for; matrix products, arithmetic and copies ran while one was open for 0% of the time, Pallas kernels for 4%

profile of v7, /device:TPU:2, one launch (start us, length us, event | category | flops | bytes accessed | tf_op | source)
XLA Modules:
  0.0 90.7 jit_solution(410269646476291795)
XLA Ops:
  0.7 73.1 %patch_net.1.gathered = bf16[24576,128]{1,0:T(8,128)(2,1)} custom-call(s32[2,16]{1,0:T(2,128)} %bitcast.6, f32[12,2,256]{2,1,0:T(2,128)} %coarse_state.1, bf16[3,3,16,128]{3,2,1,0:T(8,128)(2,1)} %w_in.1, f32[1,128]{1,0:T(1,128)} %bitcast.10, f32[1,128]{1,0:T(1,128)} %bitcast.11, f32[1,128]{1,0:T(1,128)} %bitcast.12, bf16[3,3,128,128]{3,2,1,0:T(8,128)(2,1)} %w_mid.1, ...), custom_call_target="tpu_custom_call" | custom-call | tf_op jit(solution)/shard_map/patch_net/pallas_call | solution.py:573
  73.7 3.3 %place_over.1 = bf16[13,64,256]{2,1,0:T(8,128)(2,1)} custom-call(s32[2,16]{1,0:T(2,128)} %bitcast.7, s32[1]{0:T(128)S(6)} %copy.13.count, s32[16]{0:T(128)} %blend.5, bf16[24576,128]{1,0:T(8,128)(2,1)} %patch_net.1.gathered), custom_call_target="tpu_custom_call" | custom-call | flops 402653184 | bytes 3145728 | tf_op jit(solution)/shard_map/place_over/pallas_call | solution.py:751
  77.0 1.9 %collective-permute-start = (bf16[13,64,256]{2,1,0:T(8,128)(2,1)}, bf16[13,64,256]{2,1,0:T(8,128)(2,1)S(1)}, u32[]{:S(2)}, u32[]{:S(2)}) collective-permute-start(bf16[13,64,256]{2,1,0:T(8,128)(2,1)} %place_over.1), channel_id=1, source_target_pairs={{0,8},{8,16},{16,24},{24,32},{32,40},{40,48},{48,56},{56,64},{64,7... | collective-permute-start | bytes 1277960 | tf_op jit(solution)/shard_map/ppermute | solution.py:774
  79.0 3.9 %place_own.1.num = f32[12,128,256]{2,1,0:T(8,128)} custom-call(s32[2,16]{1,0:T(2,128)} %bitcast.8, s32[1]{0:T(128)S(6)} %copy.13.count, s32[16]{0:T(128)} %blend.5, bf16[24576,128]{1,0:T(8,128)(2,1)} %patch_net.1.gathered), custom_call_target="tpu_custom_call" | custom-call | flops 805306368 | bytes 6291456 | tf_op jit(solution)/shard_map/place_own/pallas_call | solution.py:751
  82.9 4.7 %collective-permute-done.low.cover_low = bf16[13,64,256]{2,1,0:T(8,128)(2,1)S(1)} collective-permute-done((bf16[13,64,256]{2,1,0:T(8,128)(2,1)}, bf16[13,64,256]{2,1,0:T(8,128)(2,1)S(1)}, u32[]{:S(2)}, u32[]{:S(2)}) %collective-permute-start) | collective-permute-done | bytes 426016 | tf_op jit(solution)/shard_map/ppermute | solution.py:774
  87.6 0.0 copy-start
  87.6 0.8 copy-done
  88.4 2.3 %finish.1 = f32[12,128,256]{2,1,0:T(8,128)} custom-call(s32[2,16]{1,0:T(2,128)} %bitcast.9, s32[1]{0:T(128)S(6)} %copy.13.count, s32[16]{0:T(128)} %blend.5, f32[12,128,256]{2,1,0:T(8,128)} %place_own.1.num, bf16[13,64,256]{2,1,0:T(8,128)(2,1)} %copy-done, bf16[13,64,256]{2,1,0:T(8,128)(2,1)} %copy-done), custom_call_target="tpu_custom_call", output_to_operand_aliasing={{}: (3, {})} | custom-call | tf_op jit(solution)/shard_map/finish/pallas_call | solution.py:726
Async XLA Ops:
  77.0 10.6 %collective-permute-start = (bf16[13,64,256]{2,1,0:T(8,128)(2,1)}, bf16[13,64,256]{2,1,0:T(8,128)(2,1)S(1)}, u32[]{:S(2)}, u32[]{:S(2)}) collective-permute-start(bf16[13,64,256]{2,1,0:T(8,128)(2,1)} %place_over.1), channel_id=1, source_target_pairs={{0,8},{8,16},{16,24},{24,32},{32,40},{40,48},{48,56},{56,64},{64,7... | collective-permute-start | bytes 1277960 | tf_op jit(solution)/shard_map/ppermute | solution.py:774
  87.6 0.8 copy-start
